TPU v7x, 512 devices: a whole 4x4x16 slice. The times are simulated.
512 devices in a mesh: gx: 8 (over y, core), gy: 4 (over x), gz: 16 (over z).
Axes of the slice: x: 4, y: 4, z: 16, core: 2. Of those that a mesh axis runs over, the one named last changes fastest.
Arguments:
- displacement: float32 [6, 32, 32, 2048], P(None, 'gx', 'gy', 'gz'), may hold values from -6 to 6
- velocity: float32 [6, 32, 32, 2048], P(None, 'gx', 'gy', 'gz'), may hold values from -6 to 6
- moments: float32 [6, 32, 32, 2048], P(None, 'gx', 'gy', 'gz'), may hold values from -6 to 6
- sector_bit: int32 [2, 32, 32, 2048], P(None, 'gx', 'gy', 'gz'), may hold values from 0 to 1
- weight_in: bfloat16 [32, 256], replicated, may hold values from -1 to 1
- bias_in: float32 [256], replicated, may hold values from -3 to 3
- weight_mid: bfloat16 [256, 256], replicated, may hold values from -0.375 to 0.375
- weight_out: bfloat16 [256, 4], replicated, may hold values from -0.375 to 0.375
Outputs:
- displacement_out: float32 [6, 32, 32, 2048], P(None, 'gx', 'gy', 'gz')
- velocity_out: float32 [6, 32, 32, 2048], P(None, 'gx', 'gy', 'gz')
- moments_out: float32 [6, 32, 32, 2048], P(None, 'gx', 'gy', 'gz')
All inputs are finite; a program needn't handle non-finite values.
Results may differ from a plain program's by a relative error of at most 0.0014.
Values sent between devices are 32-bit elements; how exact they have to be, the bound alone decides.
A program may use at most 64 MiB of HBM per device.

v0:
```python
import jax
import jax.numpy as jnp
from jax import lax
from jax.sharding import PartitionSpec as P

half_step = 0.1
lattice_step = 0.25
second_shell = 0.5


def padded_2(block, sides, width):
    for axis, dim in sides:
        count = lax.axis_size(axis)
        forward = [(i, i + 1) for i in range(count - 1)]
        forward.append((count - 1, 0))
        backward = [(target, source) for source, target in forward]
        low = lax.ppermute(
            lax.slice_in_dim(block, block.shape[dim] - width, None, axis=dim), axis, forward
        )
        high = lax.ppermute(lax.slice_in_dim(block, 0, width, axis=dim), axis, backward)
        block = jnp.concatenate([low, block, high], axis=dim)
    return block


def rotate(moment, field, step):
    square = jnp.sum(field * field, axis=0)
    theta = step * jnp.sqrt(square)
    along = jnp.sinc(theta / jnp.pi)
    across = 0.5 * jnp.sinc(theta / (2.0 * jnp.pi)) ** 2
    cross = jnp.stack(
        [
            field[1] * moment[2] - field[2] * moment[1],
            field[2] * moment[0] - field[0] * moment[2],
            field[0] * moment[1] - field[1] * moment[0],
        ]
    )
    inner = jnp.sum(field * moment, axis=0)
    return jnp.cos(theta) * moment + step * along * cross + step * step * across * inner * field


def features_of(padded, part, sizes):
    size_x, size_y, size_z = sizes
    other = 1 - part
    sign = 2 * part - 1

    def window(first, shift_x, shift_y, shift_z):
        return padded[
            first : first + 3,
            1 + shift_x : 1 + shift_x + size_x,
            1 + shift_y : 1 + shift_y + size_y,
            1 + shift_z : 1 + shift_z + size_z,
        ]

    own_disp = window(3 * part, 0, 0, 0)
    own_spin = window(6 + 3 * part, 0, 0, 0)
    rows = []
    for corner in range(8):
        shift_x = sign * (corner >> 2 & 1)
        shift_y = sign * (corner >> 1 & 1)
        shift_z = sign * (corner & 1)
        near_disp = window(3 * other, shift_x, shift_y, shift_z)
        near_spin = window(6 + 3 * other, shift_x, shift_y, shift_z)
        rows.append(near_disp - own_disp)
        rows.append(jnp.sum(own_spin * near_spin, axis=0, keepdims=True))
    return jnp.concatenate(rows, 0)


def sector_field(spin_pad, coupling_part, part, sizes):
    other = 1 - part
    sign = 2 * part - 1
    block_shape = (3,) + sizes
    near_total = jnp.zeros(block_shape, jnp.float32)
    for corner in range(8):
        start = (
            3 * other,
            1 + sign * (corner >> 2 & 1),
            1 + sign * (corner >> 1 & 1),
            1 + sign * (corner & 1),
        )
        near_total = near_total + lax.dynamic_slice(spin_pad, start, block_shape)
    shell = jnp.zeros(block_shape, jnp.float32)
    for axis_offset in ((1, 0, 0), (-1, 0, 0), (0, 1, 0), (0, -1, 0), (0, 0, 1), (0, 0, -1)):
        start = (3 * part, 1 + axis_offset[0], 1 + axis_offset[1], 1 + axis_offset[2])
        shell = shell + lax.dynamic_slice(spin_pad, start, block_shape)
    return coupling_part[None] * near_total + second_shell * shell


def network(block, weight_in, bias_in, weight_mid, weight_out):
    dims = (((0,), (0,)), ((), ()))
    first = lax.dot_general(weight_in, block, dims, preferred_element_type=jnp.float32)
    first = jax.nn.silu(first + bias_in[:, None]).astype(jnp.bfloat16)
    second = lax.dot_general(weight_mid, first, dims, preferred_element_type=jnp.float32)
    second = jax.nn.silu(second).astype(jnp.bfloat16)
    return lax.dot_general(weight_out, second, dims, preferred_element_type=jnp.float32)


def on_device(
    displacement, velocity, moments, sector_bit, weight_in, bias_in, weight_mid, weight_out
):
    size_x, size_y, size_z = (displacement.shape[1], displacement.shape[2], displacement.shape[3])
    sizes = (size_x, size_y, size_z)
    padded = padded_2(
        jnp.concatenate([displacement, moments], 0), (("gx", 1), ("gy", 2), ("gz", 3)), 1
    )
    table_zero = features_of(padded, 0, sizes)
    table_one = features_of(padded, 1, sizes)
    width = table_zero.shape[0]
    inputs = jnp.stack([table_zero, table_one], 1).astype(jnp.bfloat16)
    blocks = inputs.reshape(width, 2 * size_x, size_y * size_z).transpose(1, 0, 2)
    result = lax.map(
        lambda block: network(block, weight_in, bias_in, weight_mid, weight_out), blocks
    )
    heads = result.transpose(1, 0, 2).reshape(4, 2, size_x, size_y, size_z)
    force = jnp.concatenate([heads[0:3, 0], heads[0:3, 1]], 0)
    coupling = 1.0 + 0.5 * jnp.tanh(heads[3])
    velocity_out = velocity + lattice_step * force
    displacement_out = displacement + lattice_step * velocity_out
    index_x = lax.axis_index("gx") * size_x + lax.broadcasted_iota(jnp.int32, sizes, 0)
    index_y = lax.axis_index("gy") * size_y + lax.broadcasted_iota(jnp.int32, sizes, 1)
    index_z = lax.axis_index("gz") * size_z + lax.broadcasted_iota(jnp.int32, sizes, 2)
    parity = (index_x + index_y + index_z) % 2
    sublattice = 4 * jnp.arange(2, dtype=jnp.int32)[:, None, None, None]
    sector_map = sublattice + 2 * sector_bit + parity[None]
    order = list(range(8)) + list(range(7, -1, -1))
    angles = [half_step] * 16
    turns = len(order)
    order_table = jnp.array(order, jnp.int32)
    angle_table = jnp.array(angles, jnp.float32)

    def rotate_sector(spins, spin_pad, sector, step):
        part = sector // 4
        own = lax.dynamic_slice_in_dim(spins, 3 * part, 3, 0)
        coupling_part = lax.dynamic_index_in_dim(coupling, part, 0, keepdims=False)
        field = sector_field(spin_pad, coupling_part, part, sizes)
        turned = rotate(own, field, step)
        chosen = lax.dynamic_index_in_dim(sector_map, part, 0, keepdims=False) == sector
        return lax.dynamic_update_slice_in_dim(
            spins, jnp.where(chosen[None], turned, own), 3 * part, 0
        )

    def sweep(turn, carry):
        spins, spin_pad = carry
        sector = order_table[turn]
        spins = rotate_sector(spins, spin_pad, sector, angle_table[turn])
        spin_pad = padded_2(spins, (("gx", 1), ("gy", 2), ("gz", 3)), 1)
        return (spins, spin_pad)

    spins, spin_pad = lax.fori_loop(0, turns - 1, sweep, (moments, padded[6:]))
    spins = rotate_sector(spins, spin_pad, order_table[turns - 1], angle_table[turns - 1])
    return (displacement_out, velocity_out, spins)


def solution(mesh):
    placed = (
        P(None, "gx", "gy", "gz"),
        P(None, "gx", "gy", "gz"),
        P(None, "gx", "gy", "gz"),
        P(None, "gx", "gy", "gz"),
        P(),
        P(),
        P(),
        P(),
    )
    return jax.shard_map(
        on_device,
        mesh=mesh,
        in_specs=placed,
        out_specs=(P(None, "gx", "gy", "gz"), P(None, "gx", "gy", "gz"), P(None, "gx", "gy", "gz")),
        check_vma=False,
    )
```

profile of v0, /device:TPU:1, one launch (start us, length us, event | category | flops | bytes accessed | tf_op | source)
XLA Modules:
  0.0 521.7 jit_solution(4703052366295636128)
XLA Ops:
  5.2 4.2 collective-permute-start.7
  16.6 4.6 collective-permute-start.9
  21.3 4.2 collective-permute-done.8
  30.4 4.6 collective-permute-start.10
  35.0 9.5 %collective-permute-start.11 = (f32[12,6,10,1]{0,3,2,1:T(1,128)S(1)}, f32[12,6,10,1]{0,3,2,1:T(1,128)S(1)}, u32[]{:S(2)}, u32[]{:S(2)}) collective-permute-start(f32[12,6,10,1]{0,3,2,1:T(1,128)S(1)} %get-tuple-element.461), channel_id=1, source_target_pairs={{1,0},{2,1},{3,2},{4,3},{5,4},{6,5},{7,6},{8,7},{9,8},{10,9},{11,1... | collective-permute-start | bytes 8648 | tf_op jit(solution)/shard_map/ppermute | solution.py:20
  51.8 8.4 %while.31 = (s32[]{:T(128)}, f32[8,4,1024]{2,1,0:T(4,128)S(1)}, bf16[8,32,1024]{2,1,0:T(8,128)(2,1)S(1)}, bf16[32,256]{1,0:T(8,128)(2,1)S(1)}, f32[256]{0:T(256)...) while((s32[]{:T(128)}, f32[8,4,1024]{2,1,0:T(4,128)S(1)}, ...), condition=%wide.region_16.17_spmd, body=%wide.region_15.0_spmd.sunk | while | flops 155975680 | bytes 1281117 | solution.py:110
  60.5 459.4 %while.32 = (s32[]{:T(128)}, f32[6,4,8,128]{3,2,1,0:T(8,128)S(1)}, f32[6,6,10,130]{3,2,1,0:T(8,128)S(1)}, s32[2,4,8,128]{3,2,1,0:T(8,128)S(1)}, f32[2,4,8,128]{3...) while((s32[]{:T(128)}, f32[6,4,8,128]{3,2,1,0:T(8,128)S(1)}, ...), condition=%wide.region_20.22_spmd.clone, body=%wide.region_17.0_spmd.sunk.clone.sunk | while | flops 1147143 | bytes 2755929 | solution.py:148
  69.0 4.6 collective-permute-start.2
  75.6 3.8 collective-permute-done.3
  79.6 3.4 collective-permute-start.4
  87.0 4.6 collective-permute-done.5
  96.4 6.6 %collective-permute-start = (f32[6,1,8,128]{3,2,1,0:T(8,128)S(1)}, f32[6,1,8,128]{3,2,1,0:T(8,128)S(1)}, u32[]{:S(2)}, u32[]{:S(2)}) collective-permute-start(f32[6,1,8,128]{3,2,1,0:T(8,128)S(1)} %get-tuple-element.612), channel_id=1, source_target_pairs={{64,0},{128,64},{192,128},{256,192},{320,256},{384,320},{448,384},... | collective-permute-start | bytes 73736 | tf_op jit(solution)/shard_map/while/body/eval_jaxpr/ppermute | solution.py:20
  106.2 3.4 collective-permute-start.3
  127.6 5.6 %collective-permute-start = (f32[6,1,8,128]{3,2,1,0:T(8,128)S(1)}, f32[6,1,8,128]{3,2,1,0:T(8,128)S(1)}, u32[]{:S(2)}, u32[]{:S(2)}) collective-permute-start(f32[6,1,8,128]{3,2,1,0:T(8,128)S(1)} %get-tuple-element.612), channel_id=1, source_target_pairs={{64,0},{128,64},{192,128},{256,192},{320,256},{384,320},{448,384},... | collective-permute-start | bytes 73736 | tf_op jit(solution)/shard_map/while/body/eval_jaxpr/ppermute | solution.py:20
  157.7 5.6 %collective-permute-start = (f32[6,1,8,128]{3,2,1,0:T(8,128)S(1)}, f32[6,1,8,128]{3,2,1,0:T(8,128)S(1)}, u32[]{:S(2)}, u32[]{:S(2)}) collective-permute-start(f32[6,1,8,128]{3,2,1,0:T(8,128)S(1)} %get-tuple-element.612), channel_id=1, source_target_pairs={{64,0},{128,64},{192,128},{256,192},{320,256},{384,320},{448,384},... | collective-permute-start | bytes 73736 | tf_op jit(solution)/shard_map/while/body/eval_jaxpr/ppermute | solution.py:20
  179.8 3.6 collective-permute-done.5
  188.3 6.1 %collective-permute-start = (f32[6,1,8,128]{3,2,1,0:T(8,128)S(1)}, f32[6,1,8,128]{3,2,1,0:T(8,128)S(1)}, u32[]{:S(2)}, u32[]{:S(2)}) collective-permute-start(f32[6,1,8,128]{3,2,1,0:T(8,128)S(1)} %get-tuple-element.612), channel_id=1, source_target_pairs={{64,0},{128,64},{192,128},{256,192},{320,256},{384,320},{448,384},... | collective-permute-start | bytes 73736 | tf_op jit(solution)/shard_map/while/body/eval_jaxpr/ppermute | solution.py:20
  211.4 3.6 collective-permute-done.5
  219.9 6.2 %collective-permute-start = (f32[6,1,8,128]{3,2,1,0:T(8,128)S(1)}, f32[6,1,8,128]{3,2,1,0:T(8,128)S(1)}, u32[]{:S(2)}, u32[]{:S(2)}) collective-permute-start(f32[6,1,8,128]{3,2,1,0:T(8,128)S(1)} %get-tuple-element.612), channel_id=1, source_target_pairs={{64,0},{128,64},{192,128},{256,192},{320,256},{384,320},{448,384},... | collective-permute-start | bytes 73736 | tf_op jit(solution)/shard_map/while/body/eval_jaxpr/ppermute | solution.py:20
  237.0 3.4 collective-permute-start.5
  250.5 5.6 %collective-permute-start = (f32[6,1,8,128]{3,2,1,0:T(8,128)S(1)}, f32[6,1,8,128]{3,2,1,0:T(8,128)S(1)}, u32[]{:S(2)}, u32[]{:S(2)}) collective-permute-start(f32[6,1,8,128]{3,2,1,0:T(8,128)S(1)} %get-tuple-element.612), channel_id=1, source_target_pairs={{64,0},{128,64},{192,128},{256,192},{320,256},{384,320},{448,384},... | collective-permute-start | bytes 73736 | tf_op jit(solution)/shard_map/while/body/eval_jaxpr/ppermute | solution.py:20
  267.1 3.4 collective-permute-start.5
  280.6 5.6 %collective-permute-start = (f32[6,1,8,128]{3,2,1,0:T(8,128)S(1)}, f32[6,1,8,128]{3,2,1,0:T(8,128)S(1)}, u32[]{:S(2)}, u32[]{:S(2)}) collective-permute-start(f32[6,1,8,128]{3,2,1,0:T(8,128)S(1)} %get-tuple-element.612), channel_id=1, source_target_pairs={{64,0},{128,64},{192,128},{256,192},{320,256},{384,320},{448,384},... | collective-permute-start | bytes 73736 | tf_op jit(solution)/shard_map/while/body/eval_jaxpr/ppermute | solution.py:20
  302.8 3.4 collective-permute-done.5
  311.0 6.1 %collective-permute-start = (f32[6,1,8,128]{3,2,1,0:T(8,128)S(1)}, f32[6,1,8,128]{3,2,1,0:T(8,128)S(1)}, u32[]{:S(2)}, u32[]{:S(2)}) collective-permute-start(f32[6,1,8,128]{3,2,1,0:T(8,128)S(1)} %get-tuple-element.612), channel_id=1, source_target_pairs={{64,0},{128,64},{192,128},{256,192},{320,256},{384,320},{448,384},... | collective-permute-start | bytes 73736 | tf_op jit(solution)/shard_map/while/body/eval_jaxpr/ppermute | solution.py:20
  342.1 6.2 %collective-permute-start = (f32[6,1,8,128]{3,2,1,0:T(8,128)S(1)}, f32[6,1,8,128]{3,2,1,0:T(8,128)S(1)}, u32[]{:S(2)}, u32[]{:S(2)}) collective-permute-start(f32[6,1,8,128]{3,2,1,0:T(8,128)S(1)} %get-tuple-element.612), channel_id=1, source_target_pairs={{64,0},{128,64},{192,128},{256,192},{320,256},{384,320},{448,384},... | collective-permute-start | bytes 73736 | tf_op jit(solution)/shard_map/while/body/eval_jaxpr/ppermute | solution.py:20
  359.3 3.4 collective-permute-start.5
  372.8 5.6 %collective-permute-start = (f32[6,1,8,128]{3,2,1,0:T(8,128)S(1)}, f32[6,1,8,128]{3,2,1,0:T(8,128)S(1)}, u32[]{:S(2)}, u32[]{:S(2)}) collective-permute-start(f32[6,1,8,128]{3,2,1,0:T(8,128)S(1)} %get-tuple-element.612), channel_id=1, source_target_pairs={{64,0},{128,64},{192,128},{256,192},{320,256},{384,320},{448,384},... | collective-permute-start | bytes 73736 | tf_op jit(solution)/shard_map/while/body/eval_jaxpr/ppermute | solution.py:20
  402.9 5.6 %collective-permute-start = (f32[6,1,8,128]{3,2,1,0:T(8,128)S(1)}, f32[6,1,8,128]{3,2,1,0:T(8,128)S(1)}, u32[]{:S(2)}, u32[]{:S(2)}) collective-permute-start(f32[6,1,8,128]{3,2,1,0:T(8,128)S(1)} %get-tuple-element.612), channel_id=1, source_target_pairs={{64,0},{128,64},{192,128},{256,192},{320,256},{384,320},{448,384},... | collective-permute-start | bytes 73736 | tf_op jit(solution)/shard_map/while/body/eval_jaxpr/ppermute | solution.py:20
  433.0 5.8 %collective-permute-start = (f32[6,1,8,128]{3,2,1,0:T(8,128)S(1)}, f32[6,1,8,128]{3,2,1,0:T(8,128)S(1)}, u32[]{:S(2)}, u32[]{:S(2)}) collective-permute-start(f32[6,1,8,128]{3,2,1,0:T(8,128)S(1)} %get-tuple-element.612), channel_id=1, source_target_pairs={{64,0},{128,64},{192,128},{256,192},{320,256},{384,320},{448,384},... | collective-permute-start | bytes 73736 | tf_op jit(solution)/shard_map/while/body/eval_jaxpr/ppermute | solution.py:20
  463.8 5.9 %collective-permute-start = (f32[6,1,8,128]{3,2,1,0:T(8,128)S(1)}, f32[6,1,8,128]{3,2,1,0:T(8,128)S(1)}, u32[]{:S(2)}, u32[]{:S(2)}) collective-permute-start(f32[6,1,8,128]{3,2,1,0:T(8,128)S(1)} %get-tuple-element.612), channel_id=1, source_target_pairs={{64,0},{128,64},{192,128},{256,192},{320,256},{384,320},{448,384},... | collective-permute-start | bytes 73736 | tf_op jit(solution)/shard_map/while/body/eval_jaxpr/ppermute | solution.py:20
  494.2 5.6 %collective-permute-start = (f32[6,1,8,128]{3,2,1,0:T(8,128)S(1)}, f32[6,1,8,128]{3,2,1,0:T(8,128)S(1)}, u32[]{:S(2)}, u32[]{:S(2)}) collective-permute-start(f32[6,1,8,128]{3,2,1,0:T(8,128)S(1)} %get-tuple-element.612), channel_id=1, source_target_pairs={{64,0},{128,64},{192,128},{256,192},{320,256},{384,320},{448,384},... | collective-permute-start | bytes 73736 | tf_op jit(solution)/shard_map/while/body/eval_jaxpr/ppermute | solution.py:20
  (452 shorter events, 329.6 us)
Async XLA Ops:
  2.5 8.8 %collective-permute-start.6 = (f32[12,1,8,128]{3,2,1,0:T(8,128)S(1)}, f32[12,1,8,128]{3,2,1,0:T(8,128)S(1)}, u32[]{:S(2)}, u32[]{:S(2)}) collective-permute-start(f32[12,1,8,128]{3,2,1,0:T(8,128)S(1)} %get-tuple-element.492), channel_id=1, source_target_pairs={{0,64},{64,128},{128,192},{192,256},{256,320},{320,384},{384,448},... | collective-permute-start | bytes 147464 | tf_op jit(solution)/shard_map/ppermute | solution.py:17
  14.6 10.8 %collective-permute-start.8 = (f32[12,6,1,128]{0,3,2,1:T(8,128)S(1)}, f32[12,6,1,128]{0,3,2,1:T(8,128)S(1)}, u32[]{:S(2)}, u32[]{:S(2)}) collective-permute-start(f32[12,6,1,128]{0,3,2,1:T(8,128)S(1)} %get-tuple-element.463), channel_id=1, source_target_pairs={{0,16},{16,32},{32,48},{48,0},{1,17},{17,33},{33,49},{49,1},{2,18}... | collective-permute-start | bytes 110600 | tf_op jit(solution)/shard_map/ppermute | solution.py:17
  16.6 9.8 %collective-permute-start.9 = (f32[12,6,1,128]{0,3,2,1:T(8,128)S(1)}, f32[12,6,1,128]{0,3,2,1:T(8,128)S(1)}, u32[]{:S(2)}, u32[]{:S(2)}) collective-permute-start(f32[12,6,1,128]{0,3,2,1:T(8,128)S(1)} %get-tuple-element.462), channel_id=1, source_target_pairs={{16,0},{32,16},{48,32},{0,48},{17,1},{33,17},{49,33},{1,49},{18,2}... | collective-permute-start | bytes 110600 | tf_op jit(solution)/shard_map/ppermute | solution.py:20
  30.4 17.8 %collective-permute-start.10 = (f32[12,6,10,1]{0,3,2,1:T(1,128)S(1)}, f32[12,6,10,1]{0,3,2,1:T(1,128)S(1)}, u32[]{:S(2)}, u32[]{:S(2)}) collective-permute-start(f32[12,6,10,1]{0,3,2,1:T(1,128)S(1)} %get-tuple-element.460), channel_id=1, source_target_pairs={{0,1},{1,2},{2,3},{3,4},{4,5},{5,6},{6,7},{7,8},{8,9},{9,10},{10,1... | collective-permute-start | bytes 8648 | tf_op jit(solution)/shard_map/ppermute | solution.py:17
  35.0 13.8 %collective-permute-start.11 = (f32[12,6,10,1]{0,3,2,1:T(1,128)S(1)}, f32[12,6,10,1]{0,3,2,1:T(1,128)S(1)}, u32[]{:S(2)}, u32[]{:S(2)}) collective-permute-start(f32[12,6,10,1]{0,3,2,1:T(1,128)S(1)} %get-tuple-element.461), channel_id=1, source_target_pairs={{1,0},{2,1},{3,2},{4,3},{5,4},{6,5},{7,6},{8,7},{9,8},{10,9},{11,1... | collective-permute-start | bytes 8648 | tf_op jit(solution)/shard_map/ppermute | solution.py:20
  79.6 7.5 %collective-permute-start.4 = (f32[6,6,10,1]{3,2,1,0:T(8,128)S(1)}, f32[6,6,10,1]{3,2,1,0:T(8,128)S(1)}, u32[]{:S(2)}, u32[]{:S(2)}) collective-permute-start(f32[6,6,10,1]{3,2,1,0:T(8,128)S(1)} %get-tuple-element.616), channel_id=1, source_target_pairs={{1,0},{2,1},{3,2},{4,3},{5,4},{6,5},{7,6},{8,7},{9,8},{10,9},{11,1... | collective-permute-start | bytes 4328 | tf_op jit(solution)/shard_map/while/body/eval_jaxpr/ppermute | solution.py:20
  82.9 8.7 %collective-permute-start.5 = (f32[6,6,10,1]{3,2,1,0:T(8,128)S(1)}, f32[6,6,10,1]{3,2,1,0:T(8,128)S(1)}, u32[]{:S(2)}, u32[]{:S(2)}) collective-permute-start(f32[6,6,10,1]{3,2,1,0:T(8,128)S(1)} %get-tuple-element.617), channel_id=1, source_target_pairs={{0,1},{1,2},{2,3},{3,4},{4,5},{5,6},{6,7},{7,8},{8,9},{9,10},{10,1... | collective-permute-start | bytes 4328 | tf_op jit(solution)/shard_map/while/body/eval_jaxpr/ppermute | solution.py:17
  96.4 7.5 %collective-permute-start = (f32[6,1,8,128]{3,2,1,0:T(8,128)S(1)}, f32[6,1,8,128]{3,2,1,0:T(8,128)S(1)}, u32[]{:S(2)}, u32[]{:S(2)}) collective-permute-start(f32[6,1,8,128]{3,2,1,0:T(8,128)S(1)} %get-tuple-element.612), channel_id=1, source_target_pairs={{64,0},{128,64},{192,128},{256,192},{320,256},{384,320},{448,384},... | collective-permute-start | bytes 73736 | tf_op jit(solution)/shard_map/while/body/eval_jaxpr/ppermute | solution.py:20
  112.2 7.5 %collective-permute-start.4 = (f32[6,6,10,1]{3,2,1,0:T(8,128)S(1)}, f32[6,6,10,1]{3,2,1,0:T(8,128)S(1)}, u32[]{:S(2)}, u32[]{:S(2)}) collective-permute-start(f32[6,6,10,1]{3,2,1,0:T(8,128)S(1)} %get-tuple-element.616), channel_id=1, source_target_pairs={{1,0},{2,1},{3,2},{4,3},{5,4},{6,5},{7,6},{8,7},{9,8},{10,9},{11,1... | collective-permute-start | bytes 4328 | tf_op jit(solution)/shard_map/while/body/eval_jaxpr/ppermute | solution.py:20
  114.1 8.7 %collective-permute-start.5 = (f32[6,6,10,1]{3,2,1,0:T(8,128)S(1)}, f32[6,6,10,1]{3,2,1,0:T(8,128)S(1)}, u32[]{:S(2)}, u32[]{:S(2)}) collective-permute-start(f32[6,6,10,1]{3,2,1,0:T(8,128)S(1)} %get-tuple-element.617), channel_id=1, source_target_pairs={{0,1},{1,2},{2,3},{3,4},{4,5},{5,6},{6,7},{7,8},{8,9},{9,10},{10,1... | collective-permute-start | bytes 4328 | tf_op jit(solution)/shard_map/while/body/eval_jaxpr/ppermute | solution.py:17
  142.3 7.5 %collective-permute-start.4 = (f32[6,6,10,1]{3,2,1,0:T(8,128)S(1)}, f32[6,6,10,1]{3,2,1,0:T(8,128)S(1)}, u32[]{:S(2)}, u32[]{:S(2)}) collective-permute-start(f32[6,6,10,1]{3,2,1,0:T(8,128)S(1)} %get-tuple-element.616), channel_id=1, source_target_pairs={{1,0},{2,1},{3,2},{4,3},{5,4},{6,5},{7,6},{8,7},{9,8},{10,9},{11,1... | collective-permute-start | bytes 4328 | tf_op jit(solution)/shard_map/while/body/eval_jaxpr/ppermute | solution.py:20
  144.2 8.7 %collective-permute-start.5 = (f32[6,6,10,1]{3,2,1,0:T(8,128)S(1)}, f32[6,6,10,1]{3,2,1,0:T(8,128)S(1)}, u32[]{:S(2)}, u32[]{:S(2)}) collective-permute-start(f32[6,6,10,1]{3,2,1,0:T(8,128)S(1)} %get-tuple-element.617), channel_id=1, source_target_pairs={{0,1},{1,2},{2,3},{3,4},{4,5},{5,6},{6,7},{7,8},{8,9},{9,10},{10,1... | collective-permute-start | bytes 4328 | tf_op jit(solution)/shard_map/while/body/eval_jaxpr/ppermute | solution.py:17
  172.4 7.5 %collective-permute-start.4 = (f32[6,6,10,1]{3,2,1,0:T(8,128)S(1)}, f32[6,6,10,1]{3,2,1,0:T(8,128)S(1)}, u32[]{:S(2)}, u32[]{:S(2)}) collective-permute-start(f32[6,6,10,1]{3,2,1,0:T(8,128)S(1)} %get-tuple-element.616), channel_id=1, source_target_pairs={{1,0},{2,1},{3,2},{4,3},{5,4},{6,5},{7,6},{8,7},{9,8},{10,9},{11,1... | collective-permute-start | bytes 4328 | tf_op jit(solution)/shard_map/while/body/eval_jaxpr/ppermute | solution.py:20
  174.8 8.7 %collective-permute-start.5 = (f32[6,6,10,1]{3,2,1,0:T(8,128)S(1)}, f32[6,6,10,1]{3,2,1,0:T(8,128)S(1)}, u32[]{:S(2)}, u32[]{:S(2)}) collective-permute-start(f32[6,6,10,1]{3,2,1,0:T(8,128)S(1)} %get-tuple-element.617), channel_id=1, source_target_pairs={{0,1},{1,2},{2,3},{3,4},{4,5},{5,6},{6,7},{7,8},{8,9},{9,10},{10,1... | collective-permute-start | bytes 4328 | tf_op jit(solution)/shard_map/while/body/eval_jaxpr/ppermute | solution.py:17
  206.4 8.7 %collective-permute-start.5 = (f32[6,6,10,1]{3,2,1,0:T(8,128)S(1)}, f32[6,6,10,1]{3,2,1,0:T(8,128)S(1)}, u32[]{:S(2)}, u32[]{:S(2)}) collective-permute-start(f32[6,6,10,1]{3,2,1,0:T(8,128)S(1)} %get-tuple-element.617), channel_id=1, source_target_pairs={{0,1},{1,2},{2,3},{3,4},{4,5},{5,6},{6,7},{7,8},{8,9},{9,10},{10,1... | collective-permute-start | bytes 4328 | tf_op jit(solution)/shard_map/while/body/eval_jaxpr/ppermute | solution.py:17
  235.1 7.5 %collective-permute-start.4 = (f32[6,6,10,1]{3,2,1,0:T(8,128)S(1)}, f32[6,6,10,1]{3,2,1,0:T(8,128)S(1)}, u32[]{:S(2)}, u32[]{:S(2)}) collective-permute-start(f32[6,6,10,1]{3,2,1,0:T(8,128)S(1)} %get-tuple-element.616), channel_id=1, source_target_pairs={{1,0},{2,1},{3,2},{4,3},{5,4},{6,5},{7,6},{8,7},{9,8},{10,9},{11,1... | collective-permute-start | bytes 4328 | tf_op jit(solution)/shard_map/while/body/eval_jaxpr/ppermute | solution.py:20
  237.0 8.7 %collective-permute-start.5 = (f32[6,6,10,1]{3,2,1,0:T(8,128)S(1)}, f32[6,6,10,1]{3,2,1,0:T(8,128)S(1)}, u32[]{:S(2)}, u32[]{:S(2)}) collective-permute-start(f32[6,6,10,1]{3,2,1,0:T(8,128)S(1)} %get-tuple-element.617), channel_id=1, source_target_pairs={{0,1},{1,2},{2,3},{3,4},{4,5},{5,6},{6,7},{7,8},{8,9},{9,10},{10,1... | collective-permute-start | bytes 4328 | tf_op jit(solution)/shard_map/while/body/eval_jaxpr/ppermute | solution.py:17
  265.2 7.5 %collective-permute-start.4 = (f32[6,6,10,1]{3,2,1,0:T(8,128)S(1)}, f32[6,6,10,1]{3,2,1,0:T(8,128)S(1)}, u32[]{:S(2)}, u32[]{:S(2)}) collective-permute-start(f32[6,6,10,1]{3,2,1,0:T(8,128)S(1)} %get-tuple-element.616), channel_id=1, source_target_pairs={{1,0},{2,1},{3,2},{4,3},{5,4},{6,5},{7,6},{8,7},{9,8},{10,9},{11,1... | collective-permute-start | bytes 4328 | tf_op jit(solution)/shard_map/while/body/eval_jaxpr/ppermute | solution.py:20
  267.1 8.7 %collective-permute-start.5 = (f32[6,6,10,1]{3,2,1,0:T(8,128)S(1)}, f32[6,6,10,1]{3,2,1,0:T(8,128)S(1)}, u32[]{:S(2)}, u32[]{:S(2)}) collective-permute-start(f32[6,6,10,1]{3,2,1,0:T(8,128)S(1)} %get-tuple-element.617), channel_id=1, source_target_pairs={{0,1},{1,2},{2,3},{3,4},{4,5},{5,6},{6,7},{7,8},{8,9},{9,10},{10,1... | collective-permute-start | bytes 4328 | tf_op jit(solution)/shard_map/while/body/eval_jaxpr/ppermute | solution.py:17
  297.5 8.7 %collective-permute-start.5 = (f32[6,6,10,1]{3,2,1,0:T(8,128)S(1)}, f32[6,6,10,1]{3,2,1,0:T(8,128)S(1)}, u32[]{:S(2)}, u32[]{:S(2)}) collective-permute-start(f32[6,6,10,1]{3,2,1,0:T(8,128)S(1)} %get-tuple-element.617), channel_id=1, source_target_pairs={{0,1},{1,2},{2,3},{3,4},{4,5},{5,6},{6,7},{7,8},{8,9},{9,10},{10,1... | collective-permute-start | bytes 4328 | tf_op jit(solution)/shard_map/while/body/eval_jaxpr/ppermute | solution.py:17
  328.6 8.7 %collective-permute-start.5 = (f32[6,6,10,1]{3,2,1,0:T(8,128)S(1)}, f32[6,6,10,1]{3,2,1,0:T(8,128)S(1)}, u32[]{:S(2)}, u32[]{:S(2)}) collective-permute-start(f32[6,6,10,1]{3,2,1,0:T(8,128)S(1)} %get-tuple-element.617), channel_id=1, source_target_pairs={{0,1},{1,2},{2,3},{3,4},{4,5},{5,6},{6,7},{7,8},{8,9},{9,10},{10,1... | collective-permute-start | bytes 4328 | tf_op jit(solution)/shard_map/while/body/eval_jaxpr/ppermute | solution.py:17
  357.4 7.5 %collective-permute-start.4 = (f32[6,6,10,1]{3,2,1,0:T(8,128)S(1)}, f32[6,6,10,1]{3,2,1,0:T(8,128)S(1)}, u32[]{:S(2)}, u32[]{:S(2)}) collective-permute-start(f32[6,6,10,1]{3,2,1,0:T(8,128)S(1)} %get-tuple-element.616), channel_id=1, source_target_pairs={{1,0},{2,1},{3,2},{4,3},{5,4},{6,5},{7,6},{8,7},{9,8},{10,9},{11,1... | collective-permute-start | bytes 4328 | tf_op jit(solution)/shard_map/while/body/eval_jaxpr/ppermute | solution.py:20
  359.3 8.7 %collective-permute-start.5 = (f32[6,6,10,1]{3,2,1,0:T(8,128)S(1)}, f32[6,6,10,1]{3,2,1,0:T(8,128)S(1)}, u32[]{:S(2)}, u32[]{:S(2)}) collective-permute-start(f32[6,6,10,1]{3,2,1,0:T(8,128)S(1)} %get-tuple-element.617), channel_id=1, source_target_pairs={{0,1},{1,2},{2,3},{3,4},{4,5},{5,6},{6,7},{7,8},{8,9},{9,10},{10,1... | collective-permute-start | bytes 4328 | tf_op jit(solution)/shard_map/while/body/eval_jaxpr/ppermute | solution.py:17
  387.5 7.5 %collective-permute-start.4 = (f32[6,6,10,1]{3,2,1,0:T(8,128)S(1)}, f32[6,6,10,1]{3,2,1,0:T(8,128)S(1)}, u32[]{:S(2)}, u32[]{:S(2)}) collective-permute-start(f32[6,6,10,1]{3,2,1,0:T(8,128)S(1)} %get-tuple-element.616), channel_id=1, source_target_pairs={{1,0},{2,1},{3,2},{4,3},{5,4},{6,5},{7,6},{8,7},{9,8},{10,9},{11,1... | collective-permute-start | bytes 4328 | tf_op jit(solution)/shard_map/while/body/eval_jaxpr/ppermute | solution.py:20
  389.4 8.7 %collective-permute-start.5 = (f32[6,6,10,1]{3,2,1,0:T(8,128)S(1)}, f32[6,6,10,1]{3,2,1,0:T(8,128)S(1)}, u32[]{:S(2)}, u32[]{:S(2)}) collective-permute-start(f32[6,6,10,1]{3,2,1,0:T(8,128)S(1)} %get-tuple-element.617), channel_id=1, source_target_pairs={{0,1},{1,2},{2,3},{3,4},{4,5},{5,6},{6,7},{7,8},{8,9},{9,10},{10,1... | collective-permute-start | bytes 4328 | tf_op jit(solution)/shard_map/while/body/eval_jaxpr/ppermute | solution.py:17
  417.6 7.5 %collective-permute-start.4 = (f32[6,6,10,1]{3,2,1,0:T(8,128)S(1)}, f32[6,6,10,1]{3,2,1,0:T(8,128)S(1)}, u32[]{:S(2)}, u32[]{:S(2)}) collective-permute-start(f32[6,6,10,1]{3,2,1,0:T(8,128)S(1)} %get-tuple-element.616), channel_id=1, source_target_pairs={{1,0},{2,1},{3,2},{4,3},{5,4},{6,5},{7,6},{8,7},{9,8},{10,9},{11,1... | collective-permute-start | bytes 4328 | tf_op jit(solution)/shard_map/while/body/eval_jaxpr/ppermute | solution.py:20
  419.5 8.7 %collective-permute-start.5 = (f32[6,6,10,1]{3,2,1,0:T(8,128)S(1)}, f32[6,6,10,1]{3,2,1,0:T(8,128)S(1)}, u32[]{:S(2)}, u32[]{:S(2)}) collective-permute-start(f32[6,6,10,1]{3,2,1,0:T(8,128)S(1)} %get-tuple-element.617), channel_id=1, source_target_pairs={{0,1},{1,2},{2,3},{3,4},{4,5},{5,6},{6,7},{7,8},{8,9},{9,10},{10,1... | collective-permute-start | bytes 4328 | tf_op jit(solution)/shard_map/while/body/eval_jaxpr/ppermute | solution.py:17
  448.4 7.5 %collective-permute-start.4 = (f32[6,6,10,1]{3,2,1,0:T(8,128)S(1)}, f32[6,6,10,1]{3,2,1,0:T(8,128)S(1)}, u32[]{:S(2)}, u32[]{:S(2)}) collective-permute-start(f32[6,6,10,1]{3,2,1,0:T(8,128)S(1)} %get-tuple-element.616), channel_id=1, source_target_pairs={{1,0},{2,1},{3,2},{4,3},{5,4},{6,5},{7,6},{8,7},{9,8},{10,9},{11,1... | collective-permute-start | bytes 4328 | tf_op jit(solution)/shard_map/while/body/eval_jaxpr/ppermute | solution.py:20
  450.3 8.7 %collective-permute-start.5 = (f32[6,6,10,1]{3,2,1,0:T(8,128)S(1)}, f32[6,6,10,1]{3,2,1,0:T(8,128)S(1)}, u32[]{:S(2)}, u32[]{:S(2)}) collective-permute-start(f32[6,6,10,1]{3,2,1,0:T(8,128)S(1)} %get-tuple-element.617), channel_id=1, source_target_pairs={{0,1},{1,2},{2,3},{3,4},{4,5},{5,6},{6,7},{7,8},{8,9},{9,10},{10,1... | collective-permute-start | bytes 4328 | tf_op jit(solution)/shard_map/while/body/eval_jaxpr/ppermute | solution.py:17
  478.8 7.5 %collective-permute-start.4 = (f32[6,6,10,1]{3,2,1,0:T(8,128)S(1)}, f32[6,6,10,1]{3,2,1,0:T(8,128)S(1)}, u32[]{:S(2)}, u32[]{:S(2)}) collective-permute-start(f32[6,6,10,1]{3,2,1,0:T(8,128)S(1)} %get-tuple-element.616), channel_id=1, source_target_pairs={{1,0},{2,1},{3,2},{4,3},{5,4},{6,5},{7,6},{8,7},{9,8},{10,9},{11,1... | collective-permute-start | bytes 4328 | tf_op jit(solution)/shard_map/while/body/eval_jaxpr/ppermute | solution.py:20
  480.7 8.7 %collective-permute-start.5 = (f32[6,6,10,1]{3,2,1,0:T(8,128)S(1)}, f32[6,6,10,1]{3,2,1,0:T(8,128)S(1)}, u32[]{:S(2)}, u32[]{:S(2)}) collective-permute-start(f32[6,6,10,1]{3,2,1,0:T(8,128)S(1)} %get-tuple-element.617), channel_id=1, source_target_pairs={{0,1},{1,2},{2,3},{3,4},{4,5},{5,6},{6,7},{7,8},{8,9},{9,10},{10,1... | collective-permute-start | bytes 4328 | tf_op jit(solution)/shard_map/while/body/eval_jaxpr/ppermute | solution.py:17
  510.8 8.7 %collective-permute-start.5 = (f32[6,6,10,1]{3,2,1,0:T(8,128)S(1)}, f32[6,6,10,1]{3,2,1,0:T(8,128)S(1)}, u32[]{:S(2)}, u32[]{:S(2)}) collective-permute-start(f32[6,6,10,1]{3,2,1,0:T(8,128)S(1)} %get-tuple-element.617), channel_id=1, source_target_pairs={{0,1},{1,2},{2,3},{3,4},{4,5},{5,6},{6,7},{7,8},{8,9},{9,10},{10,1... | collective-permute-start | bytes 4328 | tf_op jit(solution)/shard_map/while/body/eval_jaxpr/ppermute | solution.py:17
  (73 other events, 1250.4 us)
where the time goes:
time: 528 us; the launch traced here: 522 us
  starting transfers between devices  271 us (51%)
  waiting for transfers between devices  144 us (27%)
  loops' own time  41.5 us (8%)
  other arithmetic  29.5 us (6%)
  local copies, waits for them, and re-layouts  25.6 us (5%)
  matrix products  8.34 us (2%)
    ppermute x48, starting transfers between devices, padded_2(): lax.ppermute(lax.slice_in_dim(block, 0, width, axis=dim), axis, backward)  166 us
    ppermute x48, starting transfers between devices, padded_2(): lax.ppermute(lax.slice_in_dim(block, block.shape[dim] - width, None, axis...  105 us
    ppermute x48, waiting for transfers between devices, padded_2(): lax.ppermute(lax.slice_in_dim(block, block.shape[dim] - width, None, axis...  97.4 us
    ppermute x48, waiting for transfers between devices, padded_2(): lax.ppermute(lax.slice_in_dim(block, 0, width, axis=dim), axis, backward)  46.8 us
    another operation x1, loops' own time, on_device(): spins, spin_pad = lax.fori_loop(0, turns - 1, sweep, (moments, padded[6:]))  41.4 us
  transfers between devices with their start and end apart: 96, of which 77 were waited for; matrix products, arithmetic and copies ran while one was open for 1% of the time, Pallas kernels for 0%

commit v1 on v0

v1 whole, which is shorter than its diff:
```python
import functools
import itertools

import jax
import jax.numpy as jnp
from jax import lax
from jax.experimental import pallas as pl
from jax.experimental.pallas import tpu as pltpu
from jax.sharding import PartitionSpec as P

AXES = ("gx", "gy", "gz")
MESH = pl.DeviceIdType.MESH
F32 = jnp.float32
BF16 = jnp.bfloat16

DIRS = sorted(
    (d for d in itertools.product((-1, 0, 1), repeat=3) if d != (0, 0, 0)),
    key=lambda d: -sum(abs(c) for c in d),
)
UP = [d for d in DIRS if min(d) >= 0]
DOWN = [d for d in DIRS if max(d) <= 0]
GROUPS = {"d1": 3, "m1": 3, "d0": 3, "m0": 3, "c0": 2, "c1": 2, "e1": 3, "e2": 3, "e3": 3}
NAMES = list(GROUPS)


def kernel(
    disp, vel, mom, bits, w_in, bias, w_mid, w_out,
    disp_out, vel_out, mom_out,
    *scratch,
):
    n = len(NAMES)
    flat = dict(zip(NAMES, scratch[:n]))
    edge = dict(zip(NAMES, scratch[n : 2 * n]))
    strip, landed, drive, table, heads, w1, w2, w3, bias_wide, send_sem, recv_sem = scratch[2 * n :]

    size = [lax.axis_size(a) for a in AXES]
    me = [lax.axis_index(a) for a in AXES]
    beside = [
        {-1: lax.rem(i + s - 1, s), 0: i, 1: lax.rem(i + 1, s)} for i, s in zip(me, size)
    ]

    def device(d):
        return tuple(beside[k][d[k]] for k in range(3))

    barrier = pltpu.get_barrier_semaphore()
    for d in DIRS:
        pl.semaphore_signal(barrier, inc=1, device_id=device(d), device_id_type=MESH)

    row = lax.broadcasted_iota(jnp.int32, (8, 128), 0)
    lane = lax.broadcasted_iota(jnp.int32, (8, 128), 1)
    odd = (row + lane) % 2 == 1
    behind = lane % 8 >= 4
    first_lane, last_lane = lane == 0, lane == 127
    first_row, last_row = row == 0, row == 7

    def by_parity(even_plane, odd_plane):
        return jnp.where(odd, odd_plane, even_plane), jnp.where(odd, even_plane, odd_plane)

    def pack(name):
        ref = flat[name]
        total = jnp.zeros((8, 128), F32)
        j = 0
        for f in range(GROUPS[name]):
            for par in range(2):
                for i in range(2):
                    turned = ref[f, par, 2 + i, 0]
                    if j:
                        turned = pltpu.roll(turned, 8 * j, 1)
                    total = jnp.where((lane + 4) // 8 % 16 == j, turned, total)
                    j += 1
        strip[NAMES.index(name)] = total

    def copy(name, d):
        g, k = NAMES.index(name), DIRS.index(d)
        rows = {0: slice(0, 8), 1: slice(4, 8), -1: slice(0, 4)}[d[1]]
        side, tile = 1 - d[0], abs(d[1])
        if d[2]:
            src = strip.at[g, rows]
            dst = landed.at[g, side, tile, (d[2] + 1) // 2, rows]
        else:
            src = flat[name].at[:, :, 2:4, 0, rows]
            dst = flat[name].at[:, :, 2 * side : 2 * side + 2, tile, rows]
        return pltpu.make_async_remote_copy(
            src_ref=src, dst_ref=dst, send_sem=send_sem.at[g, k], recv_sem=recv_sem.at[g, k],
            device_id=device(d), device_id_type=MESH,
        )

    def send(name, dirs):
        for d in dirs:
            copy(name, d).start()

    def arrive(name, dirs):
        for d in dirs:
            copy(name, d).wait_recv()

    def sent(name, dirs=DIRS):
        for d in dirs:
            copy(name, d).wait_send()

    def unpack(name, sides=(0, 1, 2)):
        g = NAMES.index(name)
        for side in sides:
            for tile in range(2):
                both = jnp.where(behind, landed[g, side, tile, 1], landed[g, side, tile, 0])
                j = 0
                for f in range(GROUPS[name]):
                    for par in range(2):
                        for i in range(2):
                            turned = pltpu.roll(both, (128 - 8 * j) % 128, 1) if j else both
                            edge[name][f, par, 2 * side + i, tile] = turned
                            j += 1

    def load_own(name, source, first, count):
        for f in range(count):
            for i in range(2):
                pair = by_parity(source[first + f, 2 * i], source[first + f, 2 * i + 1])
                flat[name][f, 0, 2 + i, 0] = pair[0]
                flat[name][f, 1, 2 + i, 0] = pair[1]
        pack(name)

    load_own("d1", disp, 3, 3)
    load_own("m1", mom, 3, 3)
    load_own("d0", disp, 0, 3)
    load_own("m0", mom, 0, 3)
    pl.semaphore_wait(barrier, len(DIRS))
    send("m1", DIRS)
    send("d1", UP)
    send("m0", DIRS)
    send("d0", DOWN)

    w1[...] = (w_in[...].astype(F32).T * 0.5).astype(BF16)
    w2[...] = (w_mid[...].astype(F32).T * 0.5).astype(BF16)
    w3[...] = jnp.concatenate([w_out[...].astype(F32).T, jnp.zeros((12, 256), F32)], 0).astype(BF16)
    bias_wide[...] = jnp.broadcast_to(bias[...].reshape(1, 256) * 0.5, (128, 256)).T

    def shift_z(near, far, sign):
        by, last = (127, last_lane) if sign > 0 else (1, first_lane)
        axis = near.ndim - 1
        return jnp.where(last, pltpu.roll(far, by, axis), pltpu.roll(near, by, axis))

    def shift_y(near, far, sign):
        by, last = (7, last_row) if sign > 0 else (1, first_row)
        axis = near.ndim - 2
        return jnp.where(last, pltpu.roll(far, by, axis), pltpu.roll(near, by, axis))

    def odd_of(par):
        return odd if par == 0 else jnp.logical_not(odd)

    def beside_x(ref, par, i, sign):
        far = min(max(i + sign, 0), 5)
        here, there = ref[:, 1 - par, i], ref[:, 1 - par, far]
        crosses = odd_of(par) if sign > 0 else odd_of(1 - par)
        return jnp.where(crosses, there, here)

    def features(p):
        q, sign = 1 - p, 2 * p - 1
        for i in range(2):
            pair = 2 + i
            cells = {}
            for kind in ("d", "m"):
                name = kind + str(q)
                for dx in range(2):
                    for par in range(2):
                        if dx:
                            near = beside_x(flat[name], par, pair, sign)
                            far = beside_x(edge[name], par, pair, sign)
                        else:
                            near, far = flat[name][:, par, pair], edge[name][:, par, pair]
                        cells[kind, dx, par, 0] = near
                        cells[kind, dx, 1 - par, 1] = shift_z(near, far, sign)
            for par in range(2):
                own_d = flat["d" + str(p)][:, par, pair, 0]
                own_m = flat["m" + str(p)][:, par, pair, 0]
                at = (par * 2 + i) * 8
                for o in range(8):
                    dx, dy, dz = o // 4, o // 2 % 2, o % 2
                    held = (par + dy) % 2
                    near_d, near_m = cells["d", dx, held, dz], cells["m", dx, held, dz]
                    if dy:
                        near_d = shift_y(near_d[:, 0], near_d[:, 1], sign)
                        near_m = shift_y(near_m[:, 0], near_m[:, 1], sign)
                    else:
                        near_d, near_m = near_d[:, 0], near_m[:, 0]
                    diff = near_d - own_d
                    for k in range(3):
                        table[pl.ds((4 * o + k) * 32 + at, 8), :] = diff[k]
                    table[pl.ds((4 * o + 3) * 32 + at, 8), :] = jnp.sum(own_m * near_m, axis=0)

    def network(p):
        @pl.loop(0, 8)
        def _(chunk):
            x = jnp.concatenate(
                [table[pl.ds(chunk * 4 + r, 32, stride=32), :] for r in range(4)], axis=1
            ).astype(BF16)
            wide = jnp.concatenate([bias_wide[...]] * 4, axis=1)
            h = jnp.dot(w1[...], x, preferred_element_type=F32) + wide
            h = (h + h * jnp.tanh(h)).astype(BF16)
            h = jnp.dot(w2[...], h, preferred_element_type=F32)
            h = (h + h * jnp.tanh(h)).astype(BF16)
            h = jnp.dot(w3[...], h, preferred_element_type=F32)
            for r in range(4):
                heads[pl.ds((chunk * 4 + r) * 8, 8), :] = h[0:8, 128 * r : 128 * r + 128]

        def head(k, par, i):
            return heads[pl.ds((par * 2 + i) * 64 + k, 8, stride=8), :]

        name = "c" + str(p)
        for i in range(2):
            for k in range(3):
                planes = by_parity(head(k, 0, i), head(k, 1, i))
                for x in range(2):
                    v = vel[3 * p + k, 2 * i + x] + 0.25 * planes[x]
                    vel_out[3 * p + k, 2 * i + x] = v
                    disp_out[3 * p + k, 2 * i + x] = disp[3 * p + k, 2 * i + x] + 0.25 * v
            for par in range(2):
                flat[name][0, par, 2 + i, 0] = 1.0 + 0.5 * jnp.tanh(head(3, par, i))
            pair = by_parity(bits[p, 2 * i].astype(F32), bits[p, 2 * i + 1].astype(F32))
            for par in range(2):
                flat[name][1, par, 2 + i, 0] = pair[par]
        pack(name)
        send(name, DIRS)

    arrive("m1", DIRS)
    arrive("d1", UP)
    unpack("m1")
    unpack("d1", (0, 1))
    features(0)
    network(0)
    arrive("m0", DIRS)
    arrive("d0", DOWN)
    unpack("m0")
    unpack("d0", (1, 2))
    features(1)
    network(1)

    def drives(p, source):
        q, sign = 1 - p, 2 * p - 1
        name = "c" + str(p)

        def body(i):
            for k in range(3):
                along = []
                for par in range(2):
                    along.append([])
                    for ref in (flat[source], edge[source]):
                        far = min(max(i + sign, 0), 5)
                        crosses = odd_of(par) if sign > 0 else odd_of(1 - par)
                        other = jnp.where(crosses, ref[k, 1 - par, far], ref[k, 1 - par, i])
                        along[par].append(ref[k, par, i] + other)
                tall = []
                for par in range(2):
                    tall.append([])
                    for z in range(2):
                        o = along[1 - par][z]
                        s = shift_y(o, jnp.stack([o[1], o[0]]), sign)
                        tall[par].append(along[par][z] + s)
                for par in range(2):
                    near = tall[par][0] + shift_z(tall[1 - par][0], tall[1 - par][1], sign)
                    far_ = tall[par][1] + shift_z(tall[1 - par][1], tall[1 - par][0], sign)
                    drive[0, k, par, i] = near * flat[name][0, par, i]
                    drive[1, k, par, i] = far_ * edge[name][0, par, i]

        for i in range(6):
            body(i)

    def turn(v, b, twice):
        square = b[0] * b[0] + b[1] * b[1] + b[2] * b[2]
        z = square * (0.0025 / 64.0)
        c = 1.0 + z * (-1 / 2 + z * (1 / 24 + z * (-1 / 720 + z * (1 / 40320 - z / 3628800))))
        s = 0.05 + z * (-0.05 / 6 + z * (0.05 / 120 + z * (-0.05 / 5040 + z * (0.05 / 362880))))
        for _ in range(3):
            s = s * c
            c = 2.0 * (c * c) - 1.0
        if twice:
            s = 2.0 * (s * c)
            c = 2.0 * (c * c) - 1.0
        q = [s * b[k] for k in range(3)]
        w = [v[k] + v[k] for k in range(3)]
        t = [q[1] * w[2] - q[2] * w[1], q[2] * w[0] - q[0] * w[2], q[0] * w[1] - q[1] * w[0]]
        r = [q[1] * t[2] - q[2] * t[1], q[2] * t[0] - q[0] * t[2], q[0] * t[1] - q[1] * t[0]]
        return [v[k] + (c * t[k] + r[k]) for k in range(3)]

    def step(p, name, sector, extent, twice=False):
        par, bit = sector % 2, float(sector // 2 % 2)
        lo, hi = {3: (0, 6), 2: (1, 5), 1: (1, 5), 0: (2, 4)}[extent]
        refs = (flat[name], edge[name])
        opened = odd_of(par)
        fields = (flat["c" + str(p)], edge["c" + str(p)])
        for i in range(lo, hi):
            inner = [[ref[k, 1 - par, i] for ref in refs] for k in range(3)]
            field = []
            for k in range(3):
                field.append([])
                for z in range(1 if extent == 0 else 2):
                    o, far = inner[k][z], inner[k][1 - z]
                    back = refs[z][k, 1 - par, max(i - 1, 0)]
                    ahead = refs[z][k, 1 - par, min(i + 1, 5)]
                    flipped = jnp.stack([o[1], o[0]])
                    total = o + jnp.where(opened, ahead, back)
                    total = total + shift_y(o, flipped, 1) + shift_y(o, flipped, -1)
                    total = total + shift_z(o, far, 1) + shift_z(o, far, -1)
                    field[k].append(0.5 * total + drive[z, k, par, i])
            for z in range(1 if extent == 0 else 2):
                own = [refs[z][k, par, i] for k in range(3)]
                b = [field[k][z] for k in range(3)]
                chosen = fields[z][1, par, i] == bit
                if extent == 0:
                    own, b, chosen = [v[0] for v in own], [v[0] for v in b], chosen[0]
                new = turn(own, b, twice)
                for k in range(3):
                    value = jnp.where(chosen, new[k], own[k])
                    if extent == 0:
                        refs[z][k, par, i, 0] = value
                    else:
                        refs[z][k, par, i] = value

    def own_to(name, source):
        flat[name][:, :, 2:4, 0] = flat[source][:, :, 2:4, 0]
        pack(name)
        send(name, DIRS)

    arrive("c0", DIRS)
    unpack("c0")
    drives(0, "m1")
    sent("m0")
    for k, sector in enumerate((0, 1, 2, 3)):
        step(0, "m0", sector, 3 - k)
    own_to("e1", "m0")
    arrive("c1", DIRS)
    unpack("c1")
    arrive("e1", DIRS)
    unpack("e1")
    drives(1, "e1")
    sent("m1")
    for k, sector in enumerate((4, 5, 6, 7)):
        step(1, "m1", sector, 3 - k, sector == 7)
    own_to("e2", "m1")
    arrive("e2", DIRS)
    unpack("e2")
    sent("e2")
    for k, sector in enumerate((6, 5, 4)):
        step(1, "e2", sector, 2 - k)
    own_to("e3", "e2")
    arrive("e3", DIRS)
    unpack("e3")
    drives(0, "e3")
    sent("e1")
    for k, sector in enumerate((3, 2, 1, 0)):
        step(0, "e1", sector, 3 - k)
    for p, name in ((0, "e1"), (1, "e2")):
        for k in range(3):
            for i in range(2):
                planes = by_parity(flat[name][k, 0, 2 + i, 0], flat[name][k, 1, 2 + i, 0])
                for x in range(2):
                    mom_out[3 * p + k, 2 * i + x] = planes[x]

    sent("d1", UP)
    sent("d0", DOWN)
    for name in ("c0", "c1", "e3"):
        sent(name)


def on_device(displacement, velocity, moments, sector_bit, weight_in, bias_in, weight_mid, weight_out):
    vmem = pl.BlockSpec(memory_space=pltpu.VMEM)
    shape = jax.ShapeDtypeStruct(displacement.shape, F32)
    count = len(NAMES)
    groups = [pltpu.VMEM((f, 2, 6, 2, 8, 128), F32) for f in GROUPS.values()]
    return pl.pallas_call(
        kernel,
        out_shape=(shape, shape, shape),
        in_specs=[vmem] * 8,
        out_specs=(vmem, vmem, vmem),
        scratch_shapes=groups
        + groups
        + [
            pltpu.VMEM((count, 8, 128), F32),
            pltpu.VMEM((count, 3, 2, 2, 8, 128), F32),
            pltpu.VMEM((2, 3, 2, 6, 2, 8, 128), F32),
            pltpu.VMEM((1024, 128), F32),
            pltpu.VMEM((256, 128), F32),
            pltpu.VMEM((256, 32), BF16),
            pltpu.VMEM((256, 256), BF16),
            pltpu.VMEM((16, 256), BF16),
            pltpu.VMEM((256, 128), F32),
            pltpu.SemaphoreType.DMA((count, len(DIRS))),
            pltpu.SemaphoreType.DMA((count, len(DIRS))),
        ],
        compiler_params=pltpu.CompilerParams(
            collective_id=0, has_side_effects=True, vmem_limit_bytes=40 * 1024 * 1024
        ),
    )(displacement, velocity, moments, sector_bit, weight_in, bias_in, weight_mid, weight_out)


def solution(mesh):
    cells = P(None, "gx", "gy", "gz")
    return jax.shard_map(
        on_device,
        mesh=mesh,
        in_specs=(cells, cells, cells, cells, P(), P(), P(), P()),
        out_specs=(cells, cells, cells),
        check_vma=False,
    )
```

time: 528 us -> 61.5 us (0.12); the launches traced: 522 us -> 61.3 us
  starting transfers between devices: 271 us -> 0 us
  waiting for transfers between devices: 144 us -> 0 us
  Pallas kernels: 0 us -> 54.2 us
  loops' own time: 41.5 us -> 0 us
  other arithmetic: 29.5 us -> 0 us
  local copies, waits for them, and re-layouts: 25.6 us -> 6.35 us
  matrix products: 8.34 us -> 0 us
    ppermute x96 -> x0, starting transfers between devices: 271 us -> none  [the longest x48 166 us: padded_2(): lax.ppermute(lax.slice_in_dim(block, 0, width, axis=dim), axis, backward)]
    ppermute x96 -> x0, waiting for transfers between devices: 144 us -> none  [the longest x48 97.4 us: padded_2(): lax.ppermute(lax.slice_in_dim(block, block.shape[dim] - width, None, axis...]
    pallas_call x0 -> x1, Pallas kernels: none -> 54.2 us  [on_device(): pl.pallas_call(kernel, out_shape=(shape, shape, shape), in_specs=[vmem] *...]
    another operation x2 -> x0, loops' own time: 41.5 us -> none  [the longest x1 41.4 us: on_device(): spins, spin_pad = lax.fori_loop(0, turns - 1, sweep, (moments, padded[6:]))]
    concatenate x33 -> x0, other arithmetic: 10 us -> none  [padded_2(): block = jnp.concatenate([low, block, high], axis=dim)]
    broadcast_in_dim x17 -> x0, other arithmetic: 9.87 us -> none  [the longest x16 9.87 us: rotate_sector(): jnp.where(chosen[None], turned, own)]
    dynamic_slice x16 -> x0, local copies, waits for them, and re-layouts: 8.8 us -> none  [the longest x15 8.79 us: sweep(): sector = order_table[turn]]
    dot_general x16 -> x0, matrix products: 8.34 us -> none  [the longest x8 4.5 us: network(): lax.dot_general(weight_out, second, dims, preferred_element_type=jnp.floa...]
  transfers between devices with their start and end apart: 96 -> 0, of which waited for: 77 -> 0; matrix products, arithmetic and copies ran while one was open for 1% -> 0% of each run, Pallas kernels for 0% -> 0%
where the time goes in v1:
time: 61.5 us; the launch traced here: 61.3 us
  Pallas kernels  54.2 us (88%)
  local copies, waits for them, and re-layouts  6.35 us (10%)
  between operations  0.69 us (1%)
    pallas_call x1, Pallas kernels, on_device(): pl.pallas_call(kernel, out_shape=(shape, shape, shape), in_specs=[vmem] *...  54.2 us
    unnamed x18, local copies, waits for them, and re-layouts  6.35 us

profile of v1, /device:TPU:1, one launch (start us, length us, event | category | flops | bytes accessed | tf_op | source)
XLA Modules:
  0.0 61.3 jit_solution(1989339433885654188)
XLA Ops:
  0.6 0.0 copy-start.6
  0.6 0.0 copy-start.5
  0.7 0.0 copy-start.4
  0.7 0.8 %copy.11.w_out = bf16[256,4]{1,0:T(8,128)(2,1)S(1)} copy(bf16[256,4]{0,1:T(4,128)(2,1)} %param.15) | data formatting | bytes 4096 | tf_op args[7]
  1.5 0.0 copy-done.6
  1.5 0.0 copy-done.5
  1.5 0.0 copy-done.4
  1.5 0.0 copy-start
  1.5 0.9 %copy-done = bf16[256,256]{1,0:T(8,128)(2,1)S(1)} copy-done((bf16[256,256]{1,0:T(8,128)(2,1)S(1)}, bf16[256,256]{1,0:T(8,128)(2,1)}, u32[]{:S(2)}) %copy-start) | copy-done | bytes 131096
  2.4 0.0 copy-start.1
  2.4 0.9 %copy-done.1 = f32[6,4,8,128]{3,2,1,0:T(8,128)S(1)} copy-done((f32[6,4,8,128]{3,2,1,0:T(8,128)S(1)}, f32[6,4,8,128]{3,2,1,0:T(8,128)}, u32[]{:S(2)}) %copy-start.1) | copy-done | bytes 98328
  3.3 0.0 copy-start.2
  3.3 0.9 %copy-done.2 = f32[6,4,8,128]{3,2,1,0:T(8,128)S(1)} copy-done((f32[6,4,8,128]{3,2,1,0:T(8,128)S(1)}, f32[6,4,8,128]{3,2,1,0:T(8,128)}, u32[]{:S(2)}) %copy-start.2) | copy-done | bytes 98328
  4.2 0.0 copy-start.3
  4.2 0.9 %copy-done.3 = f32[6,4,8,128]{3,2,1,0:T(8,128)S(1)} copy-done((f32[6,4,8,128]{3,2,1,0:T(8,128)S(1)}, f32[6,4,8,128]{3,2,1,0:T(8,128)}, u32[]{:S(2)}) %copy-start.3) | copy-done | bytes 98328
  5.1 54.2 %shard_map.103 = (f32[6,4,8,128]{3,2,1,0:T(8,128)S(1)}, f32[6,4,8,128]{3,2,1,0:T(8,128)S(1)}, f32[6,4,8,128]{3,2,1,0:T(8,128)S(1)}) custom-call(f32[6,4,8,128]{3,2,1,0:T(8,128)S(1)} %copy-done.1, f32[6,4,8,128]{3,2,1,0:T(8,128)S(1)} %copy-done.2, f32[6,4,8,128]{3,2,1,0:T(8,128)S(1)} %copy-done.3, s32[2,4,8,128]{3,2,1,0:T(8,128)S(1)} %copy-done.4, ...), custom_call_target="tpu_custom_call" | custom-call | tf_op jit(solution)/shard_map/pallas_call | solution.py:368
  59.3 0.6 %copy.15 = f32[6,4,8,128]{3,2,1,0:T(8,128)} copy(f32[6,4,8,128]{3,2,1,0:T(8,128)S(1)} %get-tuple-element.6) | data formatting | bytes 196608
  60.0 0.6 %copy.16 = f32[6,4,8,128]{3,2,1,0:T(8,128)} copy(f32[6,4,8,128]{3,2,1,0:T(8,128)S(1)} %get-tuple-element.7) | data formatting | bytes 196608
  60.6 0.6 %copy.17 = f32[6,4,8,128]{3,2,1,0:T(8,128)} copy(f32[6,4,8,128]{3,2,1,0:T(8,128)S(1)} %get-tuple-element.8) | data formatting | bytes 196608
Async XLA Ops:
  0.6 0.9 %copy-start.6 = (f32[256]{0:T(256)S(1)}, f32[256]{0:T(256)}, u32[]{:S(2)}) copy-start(f32[256]{0:T(256)} %bias.1) | copy-start | bytes 3076
  0.6 0.9 %copy-start.5 = (bf16[32,256]{1,0:T(8,128)(2,1)S(1)}, bf16[32,256]{1,0:T(8,128)(2,1)}, u32[]{:S(2)}) copy-start(bf16[32,256]{1,0:T(8,128)(2,1)} %w_in.1) | copy-start | bytes 49156
  0.7 0.9 %copy-start.4 = (s32[2,4,8,128]{3,2,1,0:T(8,128)S(1)}, s32[2,4,8,128]{3,2,1,0:T(8,128)}, u32[]{:S(2)}) copy-start(s32[2,4,8,128]{3,2,1,0:T(8,128)} %bits.1) | copy-start | bytes 98308
  1.5 0.9 %copy-start = (bf16[256,256]{1,0:T(8,128)(2,1)S(1)}, bf16[256,256]{1,0:T(8,128)(2,1)}, u32[]{:S(2)}) copy-start(bf16[256,256]{1,0:T(8,128)(2,1)} %w_mid.1) | copy-start | bytes 393220
  2.4 0.9 %copy-start.1 = (f32[6,4,8,128]{3,2,1,0:T(8,128)S(1)}, f32[6,4,8,128]{3,2,1,0:T(8,128)}, u32[]{:S(2)}) copy-start(f32[6,4,8,128]{3,2,1,0:T(8,128)} %disp.1) | copy-start | bytes 294916
  3.3 0.9 %copy-start.2 = (f32[6,4,8,128]{3,2,1,0:T(8,128)S(1)}, f32[6,4,8,128]{3,2,1,0:T(8,128)}, u32[]{:S(2)}) copy-start(f32[6,4,8,128]{3,2,1,0:T(8,128)} %vel.1) | copy-start | bytes 294916
  4.2 0.9 %copy-start.3 = (f32[6,4,8,128]{3,2,1,0:T(8,128)S(1)}, f32[6,4,8,128]{3,2,1,0:T(8,128)}, u32[]{:S(2)}) copy-start(f32[6,4,8,128]{3,2,1,0:T(8,128)} %mom.1) | copy-start | bytes 294916

commit v2 on v1

--- a/solution.py
+++ b/solution.py
@@ -19,19 +19,27 @@
 )
 UP = [d for d in DIRS if min(d) >= 0]
 DOWN = [d for d in DIRS if max(d) <= 0]
-GROUPS = {"d1": 3, "m1": 3, "d0": 3, "m0": 3, "c0": 2, "c1": 2, "e1": 3, "e2": 3, "e3": 3}
+GROUPS = {"f1": 6, "f0": 6, "m1": 3, "m0": 3, "c0": 2, "c1": 2, "e1": 3, "e2": 3, "e3": 3}
 NAMES = list(GROUPS)
 
 
 def kernel(
-    disp, vel, mom, bits, w_in, bias, w_mid, w_out,
+    disp_in, vel_in, mom_in, bits_in, w_in_in, bias_in, w_mid_in, w_out_in,
     disp_out, vel_out, mom_out,
     *scratch,
 ):
     n = len(NAMES)
     flat = dict(zip(NAMES, scratch[:n]))
     edge = dict(zip(NAMES, scratch[n : 2 * n]))
-    strip, landed, drive, table, heads, w1, w2, w3, bias_wide, send_sem, recv_sem = scratch[2 * n :]
+    strip, landed, strip_f, landed_f, drive, table, heads, w1, w2, w3, bias_wide = scratch[2 * n : 2 * n + 11]
+    disp, vel, mom, bits, w_in, bias, w_mid, w_out, in_sem, send_sem, recv_sem, send_sem_f, recv_sem_f = scratch[2 * n + 11 :]
+    given = (
+        (mom_in, mom), (disp_in, disp), (w_in_in, w_in), (bias_in, bias), (w_mid_in, w_mid),
+        (w_out_in, w_out), (vel_in, vel), (bits_in, bits),
+    )
+    loads = [pltpu.make_async_copy(a, b, in_sem.at[k]) for k, (a, b) in enumerate(given)]
+    for load in loads:
+        load.start()
 
     size = [lax.axis_size(a) for a in AXES]
     me = [lax.axis_index(a) for a in AXES]
@@ -56,81 +64,123 @@
     def by_parity(even_plane, odd_plane):
         return jnp.where(odd, odd_plane, even_plane), jnp.where(odd, even_plane, odd_plane)
 
-    def pack(name):
-        ref = flat[name]
+    def pack(ref, first, fields):
         total = jnp.zeros((8, 128), F32)
         j = 0
-        for f in range(GROUPS[name]):
+        for f in range(fields):
             for par in range(2):
                 for i in range(2):
-                    turned = ref[f, par, 2 + i, 0]
+                    turned = ref[first + f, par, 2 + i, 0]
                     if j:
                         turned = pltpu.roll(turned, 8 * j, 1)
                     total = jnp.where((lane + 4) // 8 % 16 == j, turned, total)
                     j += 1
-        strip[NAMES.index(name)] = total
-
-    def copy(name, d):
-        g, k = NAMES.index(name), DIRS.index(d)
-        rows = {0: slice(0, 8), 1: slice(4, 8), -1: slice(0, 4)}[d[1]]
-        side, tile = 1 - d[0], abs(d[1])
-        if d[2]:
-            src = strip.at[g, rows]
-            dst = landed.at[g, side, tile, (d[2] + 1) // 2, rows]
-        else:
-            src = flat[name].at[:, :, 2:4, 0, rows]
-            dst = flat[name].at[:, :, 2 * side : 2 * side + 2, tile, rows]
-        return pltpu.make_async_remote_copy(
-            src_ref=src, dst_ref=dst, send_sem=send_sem.at[g, k], recv_sem=recv_sem.at[g, k],
-            device_id=device(d), device_id_type=MESH,
-        )
-
-    def send(name, dirs):
-        for d in dirs:
-            copy(name, d).start()
-
-    def arrive(name, dirs):
-        for d in dirs:
-            copy(name, d).wait_recv()
-
-    def sent(name, dirs=DIRS):
-        for d in dirs:
-            copy(name, d).wait_send()
-
-    def unpack(name, sides=(0, 1, 2)):
+        return total
+
+    def send(name, source, first=0):
+        g, fields = NAMES.index(name), GROUPS[name]
+        strip[g] = pack(source, first, fields)
+        for d in DIRS:
+            rows = {0: slice(0, 8), 1: slice(4, 8), -1: slice(0, 4)}[d[1]]
+            side, tile = 1 - d[0], abs(d[1])
+            if d[2]:
+                src = strip.at[g, rows]
+                dst = landed.at[g, side, tile, (d[2] + 1) // 2, rows]
+            else:
+                src = source.at[first : first + fields, :, 2:4, 0, rows]
+                dst = flat[name].at[:, :, 2 * side : 2 * side + 2, tile, rows]
+            k = abs(d[2])
+            pltpu.make_async_remote_copy(
+                src_ref=src, dst_ref=dst, send_sem=send_sem.at[g, k], recv_sem=recv_sem.at[g, k],
+                device_id=device(d), device_id_type=MESH,
+            ).start()
+
+    def both_waits(name, sems):
         g = NAMES.index(name)
-        for side in sides:
+        cells, strips = flat[name].at[:, :, 0:5], landed.at[g]
+        pltpu.make_async_copy(cells, cells, sems.at[g, 0]).wait()
+        pltpu.make_async_copy(strips, strips, sems.at[g, 1]).wait()
+
+    def arrive(name):
+        both_waits(name, recv_sem)
+        unpack(name)
+
+    def sent(name):
+        both_waits(name, send_sem)
+
+    def unpack(name):
+        g = NAMES.index(name)
+        for side in range(3):
             for tile in range(2):
                 both = jnp.where(behind, landed[g, side, tile, 1], landed[g, side, tile, 0])
                 j = 0
                 for f in range(GROUPS[name]):
                     for par in range(2):
                         for i in range(2):
-                            turned = pltpu.roll(both, (128 - 8 * j) % 128, 1) if j else both
+                            turned = pltpu.roll(both, 128 - 8 * j, 1) if j else both
                             edge[name][f, par, 2 * side + i, tile] = turned
                             j += 1
 
-    def load_own(name, source, first, count):
-        for f in range(count):
-            for i in range(2):
-                pair = by_parity(source[first + f, 2 * i], source[first + f, 2 * i + 1])
-                flat[name][f, 0, 2 + i, 0] = pair[0]
-                flat[name][f, 1, 2 + i, 0] = pair[1]
-        pack(name)
-
-    load_own("d1", disp, 3, 3)
-    load_own("m1", mom, 3, 3)
-    load_own("d0", disp, 0, 3)
-    load_own("m0", mom, 0, 3)
+    def copies_f(p):
+        ref = flat["f" + str(p)]
+        for k, d in enumerate(UP if p else DOWN):
+            rows = {0: slice(0, 8), 1: slice(4, 8), -1: slice(0, 4)}[d[1]]
+            side, tile = 1 - d[0], abs(d[1])
+            if d[2]:
+                src, dst = strip_f.at[p, :, rows], landed_f.at[p, side, tile, :, rows]
+            else:
+                here = {0: slice(2, 4), 1: slice(3, 4), -1: slice(2, 3)}[d[0]]
+                there = {0: slice(2, 4), 1: slice(1, 2), -1: slice(4, 5)}[d[0]]
+                src, dst = ref.at[:, :, here, 0, rows], ref.at[:, :, there, tile, rows]
+            yield pltpu.make_async_remote_copy(
+                src_ref=src, dst_ref=dst, send_sem=send_sem_f.at[p, k], recv_sem=recv_sem_f.at[p, k],
+                device_id=device(d), device_id_type=MESH,
+            )
+
+    def arrive_f(p):
+        for c in copies_f(p):
+            c.wait_recv()
+        for side in (0, 1) if p else (1, 2):
+            for tile in range(2):
+                for kind in range(2):
+                    got = landed_f[p, side, tile, kind]
+                    j = 0
+                    for f in range(3):
+                        for par in range(2):
+                            for i in range(2):
+                                turned = pltpu.roll(got, 128 - 8 * j, 1) if j else got
+                                edge["f" + str(p)][3 * kind + f, par, 2 * side + i, tile] = turned
+                                j += 1
+
+    def load_own(p):
+        ref = flat["f" + str(p)]
+        for kind, source in enumerate((disp, mom)):
+            for f in range(3):
+                for i in range(2):
+                    pair = by_parity(source[3 * p + f, 2 * i], source[3 * p + f, 2 * i + 1])
+                    ref[3 * kind + f, 0, 2 + i, 0] = pair[0]
+                    ref[3 * kind + f, 1, 2 + i, 0] = pair[1]
+            strip_f[p, kind] = pack(ref, 3 * kind, 3)
+
+    loads[0].wait()
+    loads[1].wait()
+    load_own(1)
     pl.semaphore_wait(barrier, len(DIRS))
-    send("m1", DIRS)
-    send("d1", UP)
-    send("m0", DIRS)
-    send("d0", DOWN)
+    for c in copies_f(1):
+        c.start()
+    load_own(0)
+    for c in copies_f(0):
+        c.start()
+    for p in (1, 0):
+        send("m" + str(p), flat["f" + str(p)], 3)
+    for load in loads[2:]:
+        load.wait()
+    for p in range(2):
+        flat["m" + str(p)][:, :, 2:4, 0] = flat["f" + str(p)][3:6, :, 2:4, 0]
 
     w1[...] = (w_in[...].astype(F32).T * 0.5).astype(BF16)
     w2[...] = (w_mid[...].astype(F32).T * 0.5).astype(BF16)
-    w3[...] = jnp.concatenate([w_out[...].astype(F32).T, jnp.zeros((12, 256), F32)], 0).astype(BF16)
+    w3[...] = jnp.concatenate([w_out[...].astype(F32), jnp.zeros((12, 256), F32)], 0).astype(BF16)
     bias_wide[...] = jnp.broadcast_to(bias[...].reshape(1, 256) * 0.5, (128, 256)).T
 
     def shift_z(near, far, sign):
@@ -146,31 +196,31 @@
     def odd_of(par):
         return odd if par == 0 else jnp.logical_not(odd)
 
-    def beside_x(ref, par, i, sign):
+    def beside_x(ref, fields, par, i, sign):
         far = min(max(i + sign, 0), 5)
-        here, there = ref[:, 1 - par, i], ref[:, 1 - par, far]
+        here, there = ref[fields, 1 - par, i], ref[fields, 1 - par, far]
         crosses = odd_of(par) if sign > 0 else odd_of(1 - par)
         return jnp.where(crosses, there, here)
 
     def features(p):
-        q, sign = 1 - p, 2 * p - 1
+        name, sign = "f" + str(1 - p), 2 * p - 1
         for i in range(2):
             pair = 2 + i
             cells = {}
             for kind in ("d", "m"):
-                name = kind + str(q)
+                fields = slice(0, 3) if kind == "d" else slice(3, 6)
                 for dx in range(2):
                     for par in range(2):
                         if dx:
-                            near = beside_x(flat[name], par, pair, sign)
-                            far = beside_x(edge[name], par, pair, sign)
+                            near = beside_x(flat[name], fields, par, pair, sign)
+                            far = beside_x(edge[name], fields, par, pair, sign)
                         else:
-                            near, far = flat[name][:, par, pair], edge[name][:, par, pair]
+                            near, far = flat[name][fields, par, pair], edge[name][fields, par, pair]
                         cells[kind, dx, par, 0] = near
                         cells[kind, dx, 1 - par, 1] = shift_z(near, far, sign)
             for par in range(2):
-                own_d = flat["d" + str(p)][:, par, pair, 0]
-                own_m = flat["m" + str(p)][:, par, pair, 0]
+                own_d = flat["f" + str(p)][0:3, par, pair, 0]
+                own_m = flat["f" + str(p)][3:6, par, pair, 0]
                 at = (par * 2 + i) * 8
                 for o in range(8):
                     dx, dy, dz = o // 4, o // 2 % 2, o % 2
@@ -217,25 +267,17 @@
             pair = by_parity(bits[p, 2 * i].astype(F32), bits[p, 2 * i + 1].astype(F32))
             for par in range(2):
                 flat[name][1, par, 2 + i, 0] = pair[par]
-        pack(name)
-        send(name, DIRS)
-
-    arrive("m1", DIRS)
-    arrive("d1", UP)
-    unpack("m1")
-    unpack("d1", (0, 1))
+        send(name, flat[name])
+
+    arrive_f(1)
     features(0)
     network(0)
-    arrive("m0", DIRS)
-    arrive("d0", DOWN)
-    unpack("m0")
-    unpack("d0", (1, 2))
+    arrive_f(0)
     features(1)
     network(1)
 
     def drives(p, source):
-        q, sign = 1 - p, 2 * p - 1
-        name = "c" + str(p)
+        sign = 2 * p - 1
 
         def body(i):
             for k in range(3):
@@ -256,9 +298,9 @@
                         tall[par].append(along[par][z] + s)
                 for par in range(2):
                     near = tall[par][0] + shift_z(tall[1 - par][0], tall[1 - par][1], sign)
-                    far_ = tall[par][1] + shift_z(tall[1 - par][1], tall[1 - par][0], sign)
-                    drive[0, k, par, i] = near * flat[name][0, par, i]
-                    drive[1, k, par, i] = far_ * edge[name][0, par, i]
+                    beyond = tall[par][1] + shift_z(tall[1 - par][1], tall[1 - par][0], sign)
+                    drive[0, k, par, i] = near
+                    drive[1, k, par, i] = beyond
 
         for i in range(6):
             body(i)
@@ -299,7 +341,7 @@
                     total = o + jnp.where(opened, ahead, back)
                     total = total + shift_y(o, flipped, 1) + shift_y(o, flipped, -1)
                     total = total + shift_z(o, far, 1) + shift_z(o, far, -1)
-                    field[k].append(0.5 * total + drive[z, k, par, i])
+                    field[k].append(0.5 * total + fields[z][0, par, i] * drive[z, k, par, i])
             for z in range(1 if extent == 0 else 2):
                 own = [refs[z][k, par, i] for k in range(3)]
                 b = [field[k][z] for k in range(3)]
@@ -314,37 +356,36 @@
                     else:
                         refs[z][k, par, i] = value
 
-    def own_to(name, source):
+    def pass_on(name, source):
+        send(name, flat[source])
         flat[name][:, :, 2:4, 0] = flat[source][:, :, 2:4, 0]
-        pack(name)
-        send(name, DIRS)
-
-    arrive("c0", DIRS)
-    unpack("c0")
+
+    arrive("m1")
     drives(0, "m1")
-    sent("m0")
+    arrive("m0")
+    arrive("c0")
     for k, sector in enumerate((0, 1, 2, 3)):
         step(0, "m0", sector, 3 - k)
-    own_to("e1", "m0")
-    arrive("c1", DIRS)
-    unpack("c1")
-    arrive("e1", DIRS)
-    unpack("e1")
+    pass_on("e1", "m0")
+    arrive("c1")
+    for p in range(2):
+        for c in copies_f(p):
+            c.wait_send()
+    for name in ("m1", "m0", "c0", "c1"):
+        sent(name)
+    arrive("e1")
     drives(1, "e1")
-    sent("m1")
     for k, sector in enumerate((4, 5, 6, 7)):
         step(1, "m1", sector, 3 - k, sector == 7)
-    own_to("e2", "m1")
-    arrive("e2", DIRS)
-    unpack("e2")
-    sent("e2")
+    pass_on("e2", "m1")
+    sent("e1")
+    arrive("e2")
     for k, sector in enumerate((6, 5, 4)):
         step(1, "e2", sector, 2 - k)
-    own_to("e3", "e2")
-    arrive("e3", DIRS)
-    unpack("e3")
+    pass_on("e3", "e2")
+    sent("e2")
+    arrive("e3")
     drives(0, "e3")
-    sent("e1")
     for k, sector in enumerate((3, 2, 1, 0)):
         step(0, "e1", sector, 3 - k)
     for p, name in ((0, "e1"), (1, "e2")):
@@ -354,13 +395,14 @@
                 for x in range(2):
                     mom_out[3 * p + k, 2 * i + x] = planes[x]
 
-    sent("d1", UP)
-    sent("d0", DOWN)
-    for name in ("c0", "c1", "e3"):
-        sent(name)
+    sent("e3")
 
 
 def on_device(displacement, velocity, moments, sector_bit, weight_in, bias_in, weight_mid, weight_out):
+    given = (
+        displacement, velocity, moments, sector_bit,
+        weight_in, bias_in, weight_mid, weight_out.T,
+    )
     vmem = pl.BlockSpec(memory_space=pltpu.VMEM)
     shape = jax.ShapeDtypeStruct(displacement.shape, F32)
     count = len(NAMES)
@@ -368,13 +410,15 @@
     return pl.pallas_call(
         kernel,
         out_shape=(shape, shape, shape),
-        in_specs=[vmem] * 8,
+        in_specs=[pl.BlockSpec(memory_space=pltpu.HBM)] * 8,
         out_specs=(vmem, vmem, vmem),
         scratch_shapes=groups
         + groups
         + [
             pltpu.VMEM((count, 8, 128), F32),
             pltpu.VMEM((count, 3, 2, 2, 8, 128), F32),
+            pltpu.VMEM((2, 2, 8, 128), F32),
+            pltpu.VMEM((2, 3, 2, 2, 8, 128), F32),
             pltpu.VMEM((2, 3, 2, 6, 2, 8, 128), F32),
             pltpu.VMEM((1024, 128), F32),
             pltpu.VMEM((256, 128), F32),
@@ -382,13 +426,19 @@
             pltpu.VMEM((256, 256), BF16),
             pltpu.VMEM((16, 256), BF16),
             pltpu.VMEM((256, 128), F32),
-            pltpu.SemaphoreType.DMA((count, len(DIRS))),
-            pltpu.SemaphoreType.DMA((count, len(DIRS))),
+        ]
+        + [pltpu.VMEM(a.shape, a.dtype) for a in given]
+        + [
+            pltpu.SemaphoreType.DMA((len(given),)),
+            pltpu.SemaphoreType.DMA((count, 2)),
+            pltpu.SemaphoreType.DMA((count, 2)),
+            pltpu.SemaphoreType.DMA((2, len(UP))),
+            pltpu.SemaphoreType.DMA((2, len(UP))),
         ],
         compiler_params=pltpu.CompilerParams(
-            collective_id=0, has_side_effects=True, vmem_limit_bytes=40 * 1024 * 1024
+            collective_id=0, has_side_effects=True, vmem_limit_bytes=60 * 1024 * 1024
         ),
-    )(displacement, velocity, moments, sector_bit, weight_in, bias_in, weight_mid, weight_out)
+    )(*given)
 
 
 def solution(mesh):

time: 61.5 us -> 53.7 us (0.87)
  Pallas kernels: 54.2 us -> 49.7 us
  local copies, waits for them, and re-layouts: 6.35 us -> 3.15 us
    pallas_call x1, Pallas kernels: 54.2 us -> 49.7 us  [on_device(): pl.pallas_call(kernel, out_shape=(shape, shape, shape), in_specs=[pl.Bloc...]
    unnamed x18 -> x7, local copies, waits for them, and re-layouts: 6.35 us -> 3.15 us
where the time goes in v2:
time: 53.7 us; the launch traced here: 53.5 us
  Pallas kernels  49.7 us (93%)
  local copies, waits for them, and re-layouts  3.15 us (6%)
  between operations  0.65 us (1%)
    pallas_call x1, Pallas kernels, on_device(): pl.pallas_call(kernel, out_shape=(shape, shape, shape), in_specs=[pl.Bloc...  49.7 us
    unnamed x7, local copies, waits for them, and re-layouts  3.15 us

profile of v2, /device:TPU:1, one launch (start us, length us, event | category | flops | bytes accessed | tf_op | source)
XLA Modules:
  0.0 53.5 jit_solution(14392606964136007747)
XLA Ops:
  0.6 49.7 %shard_map.103 = (f32[6,4,8,128]{3,2,1,0:T(8,128)}, f32[6,4,8,128]{3,2,1,0:T(8,128)}, f32[6,4,8,128]{3,2,1,0:T(8,128)}) custom-call(f32[6,4,8,128]{3,2,1,0:T(8,128)} %disp_in.1, f32[6,4,8,128]{3,2,1,0:T(8,128)} %vel_in.1, f32[6,4,8,128]{3,2,1,0:T(8,128)} %mom_in.1, s32[2,4,8,128]{3,2,1,0:T(8,128)} %bits_in.1, bf16[32,256]{1,0:T(8,128)(2,1)} %w_in_in.1, ...), custom_call_target="tpu_custom_call" | custom-call | tf_op jit(solution)/shard_map/pallas_call | solution.py:410
  50.4 0.0 copy-start.1
  50.4 1.6 %copy.14 = f32[6,4,8,128]{3,2,1,0:T(8,128)} copy(f32[6,4,8,128]{3,2,1,0:T(8,128)} %get-tuple-element.6) | data formatting | bytes 196608
  51.9 0.0 copy-done.1
  52.0 0.0 copy-start
  52.0 0.6 %copy.15 = f32[6,4,8,128]{3,2,1,0:T(8,128)} copy(f32[6,4,8,128]{3,2,1,0:T(8,128)S(1)} %copy-done.1) | data formatting | bytes 196608
  52.6 0.3 copy-done
  52.9 0.6 %copy.16 = f32[6,4,8,128]{3,2,1,0:T(8,128)} copy(f32[6,4,8,128]{3,2,1,0:T(8,128)S(1)} %copy-done) | data formatting | bytes 196608
Async XLA Ops:
  50.4 1.6 %copy-start.1 = (f32[6,4,8,128]{3,2,1,0:T(8,128)S(1)}, f32[6,4,8,128]{3,2,1,0:T(8,128)}, u32[]{:S(2)}) copy-start(f32[6,4,8,128]{3,2,1,0:T(8,128)} %get-tuple-element.7) | copy-start | bytes 294916
  52.0 0.9 %copy-start = (f32[6,4,8,128]{3,2,1,0:T(8,128)S(1)}, f32[6,4,8,128]{3,2,1,0:T(8,128)}, u32[]{:S(2)}) copy-start(f32[6,4,8,128]{3,2,1,0:T(8,128)} %get-tuple-element.8) | copy-start | bytes 294916

commit v3 on v2

--- a/solution.py
+++ b/solution.py
@@ -24,18 +24,18 @@
 
 
 def kernel(
-    disp_in, vel_in, mom_in, bits_in, w_in_in, bias_in, w_mid_in, w_out_in,
-    disp_out, vel_out, mom_out,
+    disp_in, mom_in, bits_in, w_in_in, bias_in, w_mid_in, w_out_in,
+    results,
     *scratch,
 ):
     n = len(NAMES)
     flat = dict(zip(NAMES, scratch[:n]))
     edge = dict(zip(NAMES, scratch[n : 2 * n]))
     strip, landed, strip_f, landed_f, drive, table, heads, w1, w2, w3, bias_wide = scratch[2 * n : 2 * n + 11]
-    disp, vel, mom, bits, w_in, bias, w_mid, w_out, in_sem, send_sem, recv_sem, send_sem_f, recv_sem_f = scratch[2 * n + 11 :]
+    disp, mom, bits, w_in, bias, w_mid, w_out, in_sem, send_sem, recv_sem, send_sem_f, recv_sem_f = scratch[2 * n + 11 :]
     given = (
         (mom_in, mom), (disp_in, disp), (w_in_in, w_in), (bias_in, bias), (w_mid_in, w_mid),
-        (w_out_in, w_out), (vel_in, vel), (bits_in, bits),
+        (w_out_in, w_out), (bits_in, bits),
     )
     loads = [pltpu.make_async_copy(a, b, in_sem.at[k]) for k, (a, b) in enumerate(given)]
     for load in loads:
@@ -237,7 +237,7 @@
                     table[pl.ds((4 * o + 3) * 32 + at, 8), :] = jnp.sum(own_m * near_m, axis=0)
 
     def network(p):
-        @pl.loop(0, 8)
+        @pl.loop(0, 8, unroll=8)
         def _(chunk):
             x = jnp.concatenate(
                 [table[pl.ds(chunk * 4 + r, 32, stride=32), :] for r in range(4)], axis=1
@@ -259,9 +259,7 @@
             for k in range(3):
                 planes = by_parity(head(k, 0, i), head(k, 1, i))
                 for x in range(2):
-                    v = vel[3 * p + k, 2 * i + x] + 0.25 * planes[x]
-                    vel_out[3 * p + k, 2 * i + x] = v
-                    disp_out[3 * p + k, 2 * i + x] = disp[3 * p + k, 2 * i + x] + 0.25 * v
+                    results[3 * p + k, 2 * i + x] = planes[x]
             for par in range(2):
                 flat[name][0, par, 2 + i, 0] = 1.0 + 0.5 * jnp.tanh(head(3, par, i))
             pair = by_parity(bits[p, 2 * i].astype(F32), bits[p, 2 * i + 1].astype(F32))
@@ -393,25 +391,25 @@
             for i in range(2):
                 planes = by_parity(flat[name][k, 0, 2 + i, 0], flat[name][k, 1, 2 + i, 0])
                 for x in range(2):
-                    mom_out[3 * p + k, 2 * i + x] = planes[x]
+                    results[6 + 3 * p + k, 2 * i + x] = planes[x]
 
     sent("e3")
 
 
 def on_device(displacement, velocity, moments, sector_bit, weight_in, bias_in, weight_mid, weight_out):
     given = (
-        displacement, velocity, moments, sector_bit,
+        displacement, moments, sector_bit,
         weight_in, bias_in, weight_mid, weight_out.T,
     )
     vmem = pl.BlockSpec(memory_space=pltpu.VMEM)
     shape = jax.ShapeDtypeStruct(displacement.shape, F32)
     count = len(NAMES)
     groups = [pltpu.VMEM((f, 2, 6, 2, 8, 128), F32) for f in GROUPS.values()]
-    return pl.pallas_call(
+    results = pl.pallas_call(
         kernel,
-        out_shape=(shape, shape, shape),
-        in_specs=[pl.BlockSpec(memory_space=pltpu.HBM)] * 8,
-        out_specs=(vmem, vmem, vmem),
+        out_shape=jax.ShapeDtypeStruct((12,) + displacement.shape[1:], F32),
+        in_specs=[pl.BlockSpec(memory_space=pltpu.HBM)] * 7,
+        out_specs=vmem,
         scratch_shapes=groups
         + groups
         + [
@@ -439,6 +437,8 @@
             collective_id=0, has_side_effects=True, vmem_limit_bytes=60 * 1024 * 1024
         ),
     )(*given)
+    velocity_out = velocity + 0.25 * results[:6]
+    return displacement + 0.25 * velocity_out, velocity_out, results[6:]
 
 
 def solution(mesh):

time: 53.7 us -> 50 us (0.931)
  local copies, waits for them, and re-layouts: 3.15 us -> 0.01 us
  Pallas kernels: 49.7 us -> 47.5 us
  other arithmetic: 0 us -> 1.67 us
    unnamed x7 -> x4, local copies, waits for them, and re-layouts: 3.15 us -> 0.01 us
    pallas_call x1, Pallas kernels: 49.7 us -> 47.5 us  [on_device(): pl.pallas_call(kernel, out_shape=jax.ShapeDtypeStruct((12,) + displacemen...]
    add x0 -> x1, other arithmetic: none -> 1.67 us  [on_device(): return (displacement + 0.25 * velocity_out, velocity_out, results[6:])]
where the time goes in v3:
time: 50 us; the launch traced here: 49.9 us
  Pallas kernels  47.5 us (95%)
  other arithmetic  1.67 us (3%)
  between operations  0.67 us (1%)
    pallas_call x1, Pallas kernels, on_device(): pl.pallas_call(kernel, out_shape=jax.ShapeDtypeStruct((12,) + displacemen...  47.5 us
    add x1, other arithmetic, on_device(): return (displacement + 0.25 * velocity_out, velocity_out, results[6:])  1.67 us

profile of v3, /device:TPU:1, one launch (start us, length us, event | category | flops | bytes accessed | tf_op | source)
XLA Modules:
  0.0 49.9 jit_solution(643842986666436163)
XLA Ops:
  0.6 0.0 copy-start
  0.6 0.0 copy-start.1
  0.7 47.5 %shard_map.103 = f32[12,4,8,128]{3,2,1,0:T(8,128)} custom-call(f32[6,4,8,128]{3,2,1,0:T(8,128)} %disp_in.1, f32[6,4,8,128]{3,2,1,0:T(8,128)} %mom_in.1, s32[2,4,8,128]{3,2,1,0:T(8,128)} %bits_in.1, bf16[32,256]{1,0:T(8,128)(2,1)} %w_in_in.1, f32[256]{0:T(256)} %bias_in.1, bf16[256,256]{1,0:T(8,128)(2,1)} %w_mid_in.1, bf16[4,256]{1,0:T(4,128)(2,1)} %bitcast.1), custom_call_target="tpu_custom_call" | custom-call | tf_op jit(solution)/shard_map/pallas_call | solution.py:408
  48.2 0.0 copy-done
  48.2 0.0 copy-done.1
  48.2 1.7 %multiply_add_fusion = (f32[6,4,8,128]{3,2,1,0:T(8,128)}, f32[6,4,8,128]{3,2,1,0:T(8,128)}, f32[6,4,8,128]{3,2,1,0:T(8,128)}) fusion(f32[6,4,8,128]{3,2,1,0:T(8,128)S(1)} %copy-done, f32[6,4,8,128]{3,2,1,0:T(8,128)S(1)} %copy-done.1, f32[12,4,8,128]{3,2,1,0:T(8,128)} %shard_map.103), kind=kLoop, calls=%fused_computation | loop fusion | flops 98304 | bytes 688128 | tf_op jit(solution)/shard_map/add | solution.py:441
Async XLA Ops:
  0.6 47.6 %copy-start = (f32[6,4,8,128]{3,2,1,0:T(8,128)S(1)}, f32[6,4,8,128]{3,2,1,0:T(8,128)}, u32[]{:S(2)}) copy-start(f32[6,4,8,128]{3,2,1,0:T(8,128)} %disp_in.1) | copy-start | bytes 294916
  0.6 47.6 %copy-start.1 = (f32[6,4,8,128]{3,2,1,0:T(8,128)S(1)}, f32[6,4,8,128]{3,2,1,0:T(8,128)}, u32[]{:S(2)}) copy-start(f32[6,4,8,128]{3,2,1,0:T(8,128)} %param.9) | copy-start | bytes 294916

commit v4 on v3

--- a/solution.py
+++ b/solution.py
@@ -192,6 +192,16 @@
         by, last = (7, last_row) if sign > 0 else (1, first_row)
         axis = near.ndim - 2
         return jnp.where(last, pltpu.roll(far, by, axis), pltpu.roll(near, by, axis))
+
+    def wrap_y(cells, sign):
+        by, last = (7, last_row) if sign > 0 else (1, first_row)
+        turned = pltpu.roll(cells, by, 1)
+        return jnp.where(last, jnp.stack([turned[1], turned[0]]), turned)
+
+    def wrap_z(pair, sign):
+        by, last = (127, last_lane) if sign > 0 else (1, first_lane)
+        turned = [pltpu.roll(v, by, 2) for v in pair]
+        return [jnp.where(last, turned[1 - z], turned[z]) for z in range(2)]
 
     def odd_of(par):
         return odd if par == 0 else jnp.logical_not(odd)
@@ -237,19 +247,19 @@
                     table[pl.ds((4 * o + 3) * 32 + at, 8), :] = jnp.sum(own_m * near_m, axis=0)
 
     def network(p):
-        @pl.loop(0, 8, unroll=8)
+        @pl.loop(0, 4, unroll=4)
         def _(chunk):
             x = jnp.concatenate(
-                [table[pl.ds(chunk * 4 + r, 32, stride=32), :] for r in range(4)], axis=1
+                [table[pl.ds(chunk * 8 + r, 32, stride=32), :] for r in range(8)], axis=1
             ).astype(BF16)
-            wide = jnp.concatenate([bias_wide[...]] * 4, axis=1)
+            wide = jnp.concatenate([bias_wide[...]] * 8, axis=1)
             h = jnp.dot(w1[...], x, preferred_element_type=F32) + wide
             h = (h + h * jnp.tanh(h)).astype(BF16)
             h = jnp.dot(w2[...], h, preferred_element_type=F32)
             h = (h + h * jnp.tanh(h)).astype(BF16)
             h = jnp.dot(w3[...], h, preferred_element_type=F32)
-            for r in range(4):
-                heads[pl.ds((chunk * 4 + r) * 8, 8), :] = h[0:8, 128 * r : 128 * r + 128]
+            for r in range(8):
+                heads[pl.ds((chunk * 8 + r) * 8, 8), :] = h[0:8, 128 * r : 128 * r + 128]
 
         def head(k, par, i):
             return heads[pl.ds((par * 2 + i) * 64 + k, 8, stride=8), :]
@@ -291,14 +301,11 @@
                 for par in range(2):
                     tall.append([])
                     for z in range(2):
-                        o = along[1 - par][z]
-                        s = shift_y(o, jnp.stack([o[1], o[0]]), sign)
-                        tall[par].append(along[par][z] + s)
+                        tall[par].append(along[par][z] + wrap_y(along[1 - par][z], sign))
                 for par in range(2):
-                    near = tall[par][0] + shift_z(tall[1 - par][0], tall[1 - par][1], sign)
-                    beyond = tall[par][1] + shift_z(tall[1 - par][1], tall[1 - par][0], sign)
-                    drive[0, k, par, i] = near
-                    drive[1, k, par, i] = beyond
+                    other = wrap_z(tall[1 - par], sign)
+                    for z in range(2):
+                        drive[z, k, par, i] = tall[par][z] + other[z]
 
         for i in range(6):
             body(i)
@@ -331,14 +338,13 @@
             field = []
             for k in range(3):
                 field.append([])
+                up, down = wrap_z(inner[k], 1), wrap_z(inner[k], -1)
                 for z in range(1 if extent == 0 else 2):
-                    o, far = inner[k][z], inner[k][1 - z]
+                    o = inner[k][z]
                     back = refs[z][k, 1 - par, max(i - 1, 0)]
                     ahead = refs[z][k, 1 - par, min(i + 1, 5)]
-                    flipped = jnp.stack([o[1], o[0]])
                     total = o + jnp.where(opened, ahead, back)
-                    total = total + shift_y(o, flipped, 1) + shift_y(o, flipped, -1)
-                    total = total + shift_z(o, far, 1) + shift_z(o, far, -1)
+                    total = total + (wrap_y(o, 1) + wrap_y(o, -1)) + (up[z] + down[z])
                     field[k].append(0.5 * total + fields[z][0, par, i] * drive[z, k, par, i])
             for z in range(1 if extent == 0 else 2):
                 own = [refs[z][k, par, i] for k in range(3)]

time: 50 us -> 48.6 us (0.972)
  Pallas kernels: 47.5 us -> 46.1 us
    pallas_call x1, Pallas kernels: 47.5 us -> 46.1 us  [on_device(): pl.pallas_call(kernel, out_shape=jax.ShapeDtypeStruct((12,) + displacemen...]
where the time goes in v4:
time: 48.6 us; the launch traced here: 48.5 us
  Pallas kernels  46.1 us (95%)
  other arithmetic  1.67 us (3%)
  between operations  0.67 us (1%)
    pallas_call x1, Pallas kernels, on_device(): pl.pallas_call(kernel, out_shape=jax.ShapeDtypeStruct((12,) + displacemen...  46.1 us
    add x1, other arithmetic, on_device(): return (displacement + 0.25 * velocity_out, velocity_out, results[6:])  1.67 us

profile of v4, /device:TPU:1, one launch (start us, length us, event | category | flops | bytes accessed | tf_op | source)
XLA Modules:
  0.0 48.5 jit_solution(3346539856130326258)
XLA Ops:
  0.6 0.0 copy-start
  0.6 0.0 copy-start.1
  0.7 46.1 %shard_map.103 = f32[12,4,8,128]{3,2,1,0:T(8,128)} custom-call(f32[6,4,8,128]{3,2,1,0:T(8,128)} %disp_in.1, f32[6,4,8,128]{3,2,1,0:T(8,128)} %mom_in.1, s32[2,4,8,128]{3,2,1,0:T(8,128)} %bits_in.1, bf16[32,256]{1,0:T(8,128)(2,1)} %w_in_in.1, f32[256]{0:T(256)} %bias_in.1, bf16[256,256]{1,0:T(8,128)(2,1)} %w_mid_in.1, bf16[4,256]{1,0:T(4,128)(2,1)} %bitcast.1), custom_call_target="tpu_custom_call" | custom-call | tf_op jit(solution)/shard_map/pallas_call | solution.py:414
  46.8 0.0 copy-done
  46.8 0.0 copy-done.1
  46.8 1.7 %multiply_add_fusion = (f32[6,4,8,128]{3,2,1,0:T(8,128)}, f32[6,4,8,128]{3,2,1,0:T(8,128)}, f32[6,4,8,128]{3,2,1,0:T(8,128)}) fusion(f32[6,4,8,128]{3,2,1,0:T(8,128)S(1)} %copy-done, f32[6,4,8,128]{3,2,1,0:T(8,128)S(1)} %copy-done.1, f32[12,4,8,128]{3,2,1,0:T(8,128)} %shard_map.103), kind=kLoop, calls=%fused_computation | loop fusion | flops 98304 | bytes 688128 | tf_op jit(solution)/shard_map/add | solution.py:447
Async XLA Ops:
  0.6 46.1 %copy-start = (f32[6,4,8,128]{3,2,1,0:T(8,128)S(1)}, f32[6,4,8,128]{3,2,1,0:T(8,128)}, u32[]{:S(2)}) copy-start(f32[6,4,8,128]{3,2,1,0:T(8,128)} %disp_in.1) | copy-start | bytes 294916
  0.6 46.1 %copy-start.1 = (f32[6,4,8,128]{3,2,1,0:T(8,128)S(1)}, f32[6,4,8,128]{3,2,1,0:T(8,128)}, u32[]{:S(2)}) copy-start(f32[6,4,8,128]{3,2,1,0:T(8,128)} %param.9) | copy-start | bytes 294916

commit v5 on v4

--- a/solution.py
+++ b/solution.py
@@ -38,8 +38,6 @@
         (w_out_in, w_out), (bits_in, bits),
     )
     loads = [pltpu.make_async_copy(a, b, in_sem.at[k]) for k, (a, b) in enumerate(given)]
-    for load in loads:
-        load.start()
 
     size = [lax.axis_size(a) for a in AXES]
     me = [lax.axis_index(a) for a in AXES]
@@ -53,6 +51,8 @@
     barrier = pltpu.get_barrier_semaphore()
     for d in DIRS:
         pl.semaphore_signal(barrier, inc=1, device_id=device(d), device_id_type=MESH)
+    for load in loads:
+        load.start()
 
     row = lax.broadcasted_iota(jnp.int32, (8, 128), 0)
     lane = lax.broadcasted_iota(jnp.int32, (8, 128), 1)
@@ -177,6 +177,10 @@
         load.wait()
     for p in range(2):
         flat["m" + str(p)][:, :, 2:4, 0] = flat["f" + str(p)][3:6, :, 2:4, 0]
+        for i in range(2):
+            pair = by_parity(bits[p, 2 * i].astype(F32), bits[p, 2 * i + 1].astype(F32))
+            for par in range(2):
+                flat["c" + str(p)][1, par, 2 + i, 0] = pair[par]
 
     w1[...] = (w_in[...].astype(F32).T * 0.5).astype(BF16)
     w2[...] = (w_mid[...].astype(F32).T * 0.5).astype(BF16)
@@ -266,16 +270,14 @@
 
         name = "c" + str(p)
         for i in range(2):
+            for par in range(2):
+                flat[name][0, par, 2 + i, 0] = 1.0 + 0.5 * jnp.tanh(head(3, par, i))
+        send(name, flat[name])
+        for i in range(2):
             for k in range(3):
                 planes = by_parity(head(k, 0, i), head(k, 1, i))
                 for x in range(2):
                     results[3 * p + k, 2 * i + x] = planes[x]
-            for par in range(2):
-                flat[name][0, par, 2 + i, 0] = 1.0 + 0.5 * jnp.tanh(head(3, par, i))
-            pair = by_parity(bits[p, 2 * i].astype(F32), bits[p, 2 * i + 1].astype(F32))
-            for par in range(2):
-                flat[name][1, par, 2 + i, 0] = pair[par]
-        send(name, flat[name])
 
     arrive_f(1)
     features(0)
@@ -346,19 +348,36 @@
                     total = o + jnp.where(opened, ahead, back)
                     total = total + (wrap_y(o, 1) + wrap_y(o, -1)) + (up[z] + down[z])
                     field[k].append(0.5 * total + fields[z][0, par, i] * drive[z, k, par, i])
-            for z in range(1 if extent == 0 else 2):
-                own = [refs[z][k, par, i] for k in range(3)]
-                b = [field[k][z] for k in range(3)]
-                chosen = fields[z][1, par, i] == bit
+            own = [refs[0][k, par, i] for k in range(3)]
+            b = [field[k][0] for k in range(3)]
+            chosen = fields[0][1, par, i] == bit
+            if extent == 0:
+                own, b, chosen = [v[0] for v in own], [v[0] for v in b], chosen[0]
+            new = turn(own, b, twice)
+            for k in range(3):
+                value = jnp.where(chosen, new[k], own[k])
                 if extent == 0:
-                    own, b, chosen = [v[0] for v in own], [v[0] for v in b], chosen[0]
-                new = turn(own, b, twice)
-                for k in range(3):
-                    value = jnp.where(chosen, new[k], own[k])
-                    if extent == 0:
-                        refs[z][k, par, i, 0] = value
-                    else:
-                        refs[z][k, par, i] = value
+                    refs[0][k, par, i, 0] = value
+                else:
+                    refs[0][k, par, i] = value
+            if extent:
+                parts = [field[k][1] for k in range(3)] + [refs[1][k, par, i] for k in range(3)]
+                parts.append(fields[1][1, par, i])
+                if i == lo:
+                    packed = parts
+                else:
+                    here = (lane + 4) // 8 % 16 == i - lo
+                    packed = [
+                        jnp.where(here, pltpu.roll(v, 8 * (i - lo), 2), t)
+                        for v, t in zip(parts, packed)
+                    ]
+        if extent:
+            new = turn(packed[3:6], packed[:3], twice)
+            for k in range(3):
+                value = jnp.where(packed[6] == bit, new[k], packed[3 + k])
+                for i in range(lo, hi):
+                    back = (128 - 8 * (i - lo)) % 128
+                    refs[1][k, par, i] = pltpu.roll(value, back, 2) if back else value
 
     def pass_on(name, source):
         send(name, flat[source])

time: 48.6 us -> 49.4 us (1.016)
  Pallas kernels: 46.1 us -> 46.9 us
    pallas_call x1, Pallas kernels: 46.1 us -> 46.9 us  [on_device(): pl.pallas_call(kernel, out_shape=jax.ShapeDtypeStruct((12,) + displacemen...]
where the time goes in v5:
time: 49.4 us; the launch traced here: 49.2 us
  Pallas kernels  46.9 us (95%)
  other arithmetic  1.67 us (3%)
  between operations  0.67 us (1%)
    pallas_call x1, Pallas kernels, on_device(): pl.pallas_call(kernel, out_shape=jax.ShapeDtypeStruct((12,) + displacemen...  46.9 us
    add x1, other arithmetic, on_device(): return (displacement + 0.25 * velocity_out, velocity_out, results[6:])  1.67 us

profile of v5, /device:TPU:1, one launch (start us, length us, event | category | flops | bytes accessed | tf_op | source)
XLA Modules:
  0.0 49.2 jit_solution(267417571518951029)
XLA Ops:
  0.6 0.0 copy-start
  0.6 0.0 copy-start.1
  0.7 46.9 %shard_map.103 = f32[12,4,8,128]{3,2,1,0:T(8,128)} custom-call(f32[6,4,8,128]{3,2,1,0:T(8,128)} %disp_in.1, f32[6,4,8,128]{3,2,1,0:T(8,128)} %mom_in.1, s32[2,4,8,128]{3,2,1,0:T(8,128)} %bits_in.1, bf16[32,256]{1,0:T(8,128)(2,1)} %w_in_in.1, f32[256]{0:T(256)} %bias_in.1, bf16[256,256]{1,0:T(8,128)(2,1)} %w_mid_in.1, bf16[4,256]{1,0:T(4,128)(2,1)} %bitcast.1), custom_call_target="tpu_custom_call" | custom-call | tf_op jit(solution)/shard_map/pallas_call | solution.py:433
  47.5 0.0 copy-done
  47.5 0.0 copy-done.1
  47.6 1.7 %multiply_add_fusion = (f32[6,4,8,128]{3,2,1,0:T(8,128)}, f32[6,4,8,128]{3,2,1,0:T(8,128)}, f32[6,4,8,128]{3,2,1,0:T(8,128)}) fusion(f32[6,4,8,128]{3,2,1,0:T(8,128)S(1)} %copy-done, f32[6,4,8,128]{3,2,1,0:T(8,128)S(1)} %copy-done.1, f32[12,4,8,128]{3,2,1,0:T(8,128)} %shard_map.103), kind=kLoop, calls=%fused_computation | loop fusion | flops 98304 | bytes 688128 | tf_op jit(solution)/shard_map/add | solution.py:466
Async XLA Ops:
  0.6 46.9 %copy-start = (f32[6,4,8,128]{3,2,1,0:T(8,128)S(1)}, f32[6,4,8,128]{3,2,1,0:T(8,128)}, u32[]{:S(2)}) copy-start(f32[6,4,8,128]{3,2,1,0:T(8,128)} %disp_in.1) | copy-start | bytes 294916
  0.6 46.9 %copy-start.1 = (f32[6,4,8,128]{3,2,1,0:T(8,128)S(1)}, f32[6,4,8,128]{3,2,1,0:T(8,128)}, u32[]{:S(2)}) copy-start(f32[6,4,8,128]{3,2,1,0:T(8,128)} %param.9) | copy-start | bytes 294916
